TPU v7x, 128 devices: a whole 4x4x4 slice. The times are simulated.
128 devices in a mesh: lon: 32 (over z_hi, x, y), lat: 4 (over z_lo, core).
Axes of the slice: x: 4, y: 4, z: 4 (z_hi: 2, z_lo: 2; z = z_hi * 2 + z_lo), core: 2. Of those that a mesh axis runs over, the one named last changes fastest.
Arguments:
- tokens: bfloat16 [64, 512, 1536], P('lat', 'lon'), may hold values from -48 to 48
- qkv_weight: bfloat16 [1536, 4608], replicated, may hold values from -0.15625 to 0.15625
- rel_bias: float32 [24, 15, 15], replicated, may hold values from -4 to 4
- proj_weight: bfloat16 [1536, 1536], replicated, may hold values from -0.15625 to 0.15625
- norm_gain: float32 [1536], replicated, may hold values from 0.1 to 1.9
- norm_shift: float32 [1536], replicated, may hold values from -3 to 3
- cotangent: bfloat16 [64, 512, 1536], P('lat', 'lon'), may hold values from -40 to 40
Outputs:
- out: bfloat16 [64, 512, 1536], P('lat', 'lon')
- d_tokens: bfloat16 [64, 512, 1536], P('lat', 'lon')
- d_proj_weight: float32 [1536, 1536], P(('lon', 'lat'))
- d_rel_bias: float32 [24, 15, 15], replicated
- d_norm_gain: float32 [1536], replicated
- d_norm_shift: float32 [1536], replicated
All inputs are finite; a program needn't handle non-finite values.
Results may differ from a plain program's by a relative error of at most 0.015.
The roundings to bfloat16 on the way count: a program that leaves them out, or rounds other values in their place, can miss the bound.
Values may be sent and summed in bfloat16 or wider, within the bound.
A program may use at most 128 MiB of HBM per device.

v0:
```python
import jax
import jax.numpy as jnp
from jax import lax
from jax.sharding import PartitionSpec as P

WIN = 8
PARAMS = 2367768


norm_epsilon = 1e-05
clip_epsilon = 1e-06


def from_behind(value, axis, steps):
    count = lax.axis_size(axis)
    pairs = [(source, (source + steps) % count) for source in range(count)]
    return lax.ppermute(value, axis, pairs)


def offset_onehot(window):
    places = jnp.arange(window * window, dtype=jnp.int32)
    row_of = places // window
    column_of = places % window
    rel_rows = row_of[:, None] - row_of[None, :] + window - 1
    rel_columns = column_of[:, None] - column_of[None, :] + window - 1
    slot_ids = (rel_rows * (2 * window - 1) + rel_columns).reshape(-1)
    targets = jnp.arange((2 * window - 1) * (2 * window - 1), dtype=jnp.int32)
    return (slot_ids[:, None] == targets[None, :]).astype(jnp.float32)


def to_windows(block_grid, window):
    lat_rows, lon_cols, channels = block_grid.shape
    grid_cells = block_grid.reshape(
        lat_rows // window, window, lon_cols // window, window, channels
    )
    return grid_cells.transpose(0, 2, 1, 3, 4).reshape(lat_rows * lon_cols, channels)


def from_windows(flat_rows, lat_rows, lon_cols, window):
    channels = flat_rows.shape[-1]
    grid_cells = flat_rows.reshape(lat_rows // window, lon_cols // window, window, window, channels)
    return grid_cells.transpose(0, 2, 1, 3, 4).reshape(lat_rows, lon_cols, channels)


def slide_columns(front_part, back_part, step_by):
    return from_behind((front_part, back_part), "lon", step_by)


def slide_rows(front_part, back_part, step_by):
    return from_behind((front_part, back_part), "lat", step_by)


def on_device(tokens, qkv_weight, rel_bias, proj_weight, norm_gain, norm_shift, cotangent):
    half_window = WIN // 2
    lat_rows, lon_cols, channels = tokens.shape
    head_count = rel_bias.shape[0]
    head_size = channels // head_count
    window_cells = WIN * WIN
    windows = lat_rows * lon_cols // window_cells
    score_scale = float(head_size) ** (-0.5)
    span_cells = rel_bias.shape[1] * rel_bias.shape[2]
    came_x, came_cot = slide_columns(tokens[:, :half_window], cotangent[:, :half_window], -1)
    wide_x = jnp.concatenate([tokens[:, half_window:], came_x], axis=1)
    wide_cot = jnp.concatenate([cotangent[:, half_window:], came_cot], axis=1)
    came_x, came_cot = slide_rows(wide_x[:half_window], wide_cot[:half_window], -1)
    local_x = jnp.concatenate([wide_x[half_window:], came_x], axis=0)
    local_cot = jnp.concatenate([wide_cot[half_window:], came_cot], axis=0)
    flat_x = to_windows(local_x, WIN)
    flat_cot = to_windows(local_cot, WIN)
    onehot = offset_onehot(WIN)
    position_bias = jnp.dot(
        rel_bias.reshape(head_count, span_cells), onehot.T, precision=lax.Precision.HIGHEST
    ).reshape(head_count, window_cells, window_cells)
    band_of = jnp.arange(windows, dtype=jnp.int32) // (lon_cols // WIN)
    final_band = (band_of == lat_rows // WIN - 1) & (
        lax.axis_index("lat") == lax.axis_size("lat") - 1
    )
    upper_half = jnp.arange(window_cells, dtype=jnp.int32) // WIN < half_window
    same_region = upper_half[:, None] == upper_half[None, :]
    allowed = same_region[None, None] | jnp.logical_not(final_band)[:, None, None, None]

    def split_heads(flat_rows):
        return flat_rows.reshape(windows, window_cells, head_count, head_size)

    packed_heads = jnp.dot(flat_x, qkv_weight, preferred_element_type=jnp.float32).astype(
        jnp.bfloat16
    )
    query = split_heads(packed_heads[:, :channels])
    key_part = split_heads(packed_heads[:, channels : 2 * channels])
    value_part = split_heads(packed_heads[:, 2 * channels :])
    scores = (
        jnp.einsum("wihe,wjhe->whij", query, key_part, preferred_element_type=jnp.float32)
        * score_scale
        + position_bias[None]
    )
    scores = jnp.where(allowed, scores, -jnp.inf)
    row_peak = jnp.max(scores, axis=-1, keepdims=True)
    raised = jnp.exp(scores - row_peak)
    shares = raised / jnp.sum(raised, axis=-1, keepdims=True)
    shares_low = shares.astype(jnp.bfloat16)
    mixed_heads = (
        jnp.einsum("whij,wjhe->wihe", shares_low, value_part, preferred_element_type=jnp.float32)
        .reshape(-1, channels)
        .astype(jnp.bfloat16)
    )
    projected = jnp.dot(mixed_heads, proj_weight, preferred_element_type=jnp.float32)
    centre = projected - jnp.mean(projected, axis=-1, keepdims=True)
    inverse = lax.rsqrt(jnp.mean(centre * centre, axis=-1, keepdims=True) + norm_epsilon)
    normed = centre * inverse
    out_flat = (flat_x.astype(jnp.float32) + normed * norm_gain + norm_shift).astype(jnp.bfloat16)
    upstream = flat_cot.astype(jnp.float32)
    part_gain = jnp.sum(upstream * normed, axis=0)
    part_shift = jnp.sum(upstream, axis=0)
    d_normed = upstream * norm_gain
    d_proj = (
        inverse
        * (
            d_normed
            - jnp.mean(d_normed, axis=-1, keepdims=True)
            - normed * jnp.mean(d_normed * normed, axis=-1, keepdims=True)
        )
    ).astype(jnp.bfloat16)
    d_mixed = lax.dot_general(
        d_proj, proj_weight, (((1,), (1,)), ((), ())), preferred_element_type=jnp.float32
    ).astype(jnp.bfloat16)
    d_mixed_heads = split_heads(d_mixed)
    d_shares = jnp.einsum(
        "wihe,wjhe->whij", d_mixed_heads, value_part, preferred_element_type=jnp.float32
    )
    d_scores = shares * (d_shares - jnp.sum(shares * d_shares, axis=-1, keepdims=True))
    part_bias = jnp.sum(d_scores, axis=0).reshape(head_count, window_cells * window_cells)
    d_scores_low = d_scores.astype(jnp.bfloat16)
    d_query = (
        jnp.einsum("whij,wjhe->wihe", d_scores_low, key_part, preferred_element_type=jnp.float32)
        * score_scale
    )
    d_key = (
        jnp.einsum("whij,wihe->wjhe", d_scores_low, query, preferred_element_type=jnp.float32)
        * score_scale
    )
    d_value = jnp.einsum(
        "whij,wihe->wjhe", shares_low, d_mixed_heads, preferred_element_type=jnp.float32
    )
    d_qkv = jnp.concatenate(
        [d_query.reshape(-1, channels), d_key.reshape(-1, channels), d_value.reshape(-1, channels)],
        axis=1,
    ).astype(jnp.bfloat16)
    d_flat = (
        upstream
        + lax.dot_general(
            d_qkv, qkv_weight, (((1,), (1,)), ((), ())), preferred_element_type=jnp.float32
        )
    ).astype(jnp.bfloat16)
    local_rel = jnp.dot(part_bias, onehot, precision=lax.Precision.HIGHEST)
    small_sums = lax.psum((local_rel, part_gain, part_shift), ("lon", "lat"))
    summed = lax.psum_scatter(
        lax.dot_general(
            mixed_heads, d_proj, (((0,), (0,)), ((), ())), preferred_element_type=jnp.float32
        ),
        ("lon", "lat"),
        scatter_dimension=0,
        tiled=True,
    )
    shard_squares = jnp.sum(summed * summed)
    spread_squares = lax.psum(shard_squares, ("lon", "lat"))
    rel_sum, gain_sum, shift_sum = small_sums
    squares = (
        spread_squares
        + jnp.sum(rel_sum * rel_sum)
        + jnp.sum(gain_sum * gain_sum)
        + jnp.sum(shift_sum * shift_sum)
    )
    factor = jnp.minimum(1.0, jnp.sqrt(PARAMS / (squares + clip_epsilon)))
    out_block = from_windows(out_flat, lat_rows, lon_cols, WIN)
    grad_block = from_windows(d_flat, lat_rows, lon_cols, WIN)
    came_out, came_grad = slide_rows(out_block[-half_window:], grad_block[-half_window:], 1)
    rows_out = jnp.concatenate([came_out, out_block[:-half_window]], axis=0)
    rows_grad = jnp.concatenate([came_grad, grad_block[:-half_window]], axis=0)
    came_out, came_grad = slide_columns(rows_out[:, -half_window:], rows_grad[:, -half_window:], 1)
    final_out = jnp.concatenate([came_out, rows_out[:, :-half_window]], axis=1)
    final_grad = jnp.concatenate([came_grad, rows_grad[:, :-half_window]], axis=1)
    return (
        final_out,
        final_grad,
        summed * factor,
        (rel_sum * factor).reshape(rel_bias.shape),
        gain_sum * factor,
        shift_sum * factor,
    )


def solution(mesh):
    in_specs = (P("lat", "lon", None), P(), P(), P(), P(), P(), P("lat", "lon", None))
    out_specs = (
        P("lat", "lon", None),
        P("lat", "lon", None),
        P(("lon", "lat"), None),
        P(),
        P(),
        P(),
    )
    return jax.shard_map(
        on_device, mesh=mesh, in_specs=in_specs, out_specs=out_specs, check_vma=False
    )
```

profile of v0, /device:TPU:0, one launch (start us, length us, event | category | flops | bytes accessed | tf_op | source)
XLA Modules:
  0.0 765.1 jit_solution(14770356048304552586)
XLA Ops:
  1.8 10.2 %collective-permute-start.4 = (bf16[16,4,1536]{2,1,0:T(4,128)(2,1)S(1)}, bf16[16,4,1536]{2,1,0:T(4,128)(2,1)S(1)}, u32[]{:S(2)}, u32[]{:S(2)}) collective-permute-start(bf16[16,4,1536]{2,1,0:T(4,128)(2,1)S(1)} %slice.69), channel_id=1, source_target_pairs={{0,124},{4,0},{8,4},{12,8},{16,12},{20,16},{24,20},{28,24},{32,28}... | collective-permute-start | bytes 589832 | tf_op jit(solution)/shard_map/ppermute | solution.py:17
  13.1 9.0 %collective-permute-start = (bf16[16,4,1536]{2,1,0:T(4,128)(2,1)S(1)}, bf16[16,4,1536]{2,1,0:T(4,128)(2,1)S(1)}, u32[]{:S(2)}, u32[]{:S(2)}) collective-permute-start(bf16[16,4,1536]{2,1,0:T(4,128)(2,1)S(1)} %slice.58), channel_id=1, source_target_pairs={{0,124},{4,0},{8,4},{12,8},{16,12},{20,16},{24,20},{28,24},{32,28}... | collective-permute-start | bytes 589832 | tf_op jit(solution)/shard_map/ppermute | solution.py:17
  24.5 2.7 convolution_bitcast_fusion
  30.5 9.5 %collective-permute-start.5 = (bf16[4,16,1536]{2,1,0:T(8,128)(2,1)S(1)}, bf16[4,16,1536]{2,1,0:T(8,128)(2,1)S(1)}, u32[]{:S(2)}, u32[]{:S(2)}) collective-permute-start(bf16[4,16,1536]{2,1,0:T(8,128)(2,1)S(1)} %pad_maximum_fusion.4), channel_id=1, source_target_pairs={{0,3},{1,0},{2,1},{3,2},{4,7},{5,4},{6,5},{7,6},{8,11},{9,8},{10,9... | collective-permute-start | bytes 589832 | tf_op jit(solution)/shard_map/ppermute | solution.py:17
  41.4 1.8 collective-permute-done.5
  44.8 9.2 %convolution_convert_fusion = bf16[256,4608]{1,0:T(8,128)(2,1)S(1)} fusion(bf16[256,1536]{1,0:T(8,128)(2,1)S(1)} %bitcast.72, bf16[1536,4608]{1,0:T(8,128)(2,1)} %param.8), kind=kOutput, calls=%fused_computation.1 | convolution fusion | flops 3625058304 | bytes 17301504 | tf_op jit(solution)/shard_map/dot_general | solution.py:85
  55.5 2.4 reshape.250
  57.9 1.8 copy.97
  59.7 3.1 reshape.248
  62.8 2.4 reshape.249
  65.2 1.9 copy.101
  67.1 5.4 fusion.39
  72.5 3.8 fusion.17
  76.3 2.0 copy.91
  78.3 2.2 convert_element_type.60
  80.5 4.0 fusion.40
  87.7 4.8 convolution_convert_fusion.1
  92.4 5.1 fusion.41
  97.5 378.1 %fusion = f32[16,1536]{1,0:T(8,128)S(1)} fusion(f32[1536,1536]{1,0:T(8,128)} %fusion.41), kind=kCustom, calls=%all-reduce-scatter | all-reduce-scatter fusion | flops 3145729 | bytes 9535488
  475.6 1.9 collective-permute-start.38
  477.5 1.9 collective-permute-start.37
  479.5 1.9 collective-permute-start.36
  481.4 1.9 collective-permute-start.35
  483.3 2.4 reshape.254
  485.7 1.8 copy.105
  489.0 3.9 multiply_reduce_fusion
  495.5 2.1 fusion.24
  499.1 14.4 %collective-permute-start.31 = (f32[16,1536]{1,0:T(8,128)S(1)}, f32[16,1536]{1,0:T(8,128)S(1)}, u32[]{:S(2)}, u32[]{:S(2)}) collective-permute-start(f32[16,1536]{1,0:T(8,128)S(1)} %fusion), channel_id=1, source_target_pairs={{0,24},{1,25},{2,26},{3,27},{4,28},{5,29},{6,30},{7,31},{8,32},{9,... | collective-permute-start | bytes 294920
  513.5 2.3 collective-permute-start.30
  515.8 5.4 collective-permute-start.29
  522.5 2.1 fusion.18
  526.0 1.6 collective-permute-start.26
  527.7 1.7 collective-permute-start.25
  530.8 3.6 collective-permute-start.23
  534.4 2.1 fusion.20
  536.6 5.6 collective-permute-start.22
  542.2 1.9 collective-permute-start.21
  544.2 2.3 collective-permute-start.20
  546.4 2.2 collective-permute-start.19
  548.6 3.3 collective-permute-start.18
  552.0 2.2 fusion.19
  554.1 2.2 copy.107
  556.3 1.7 reshape.257
  558.0 2.4 copy.100
  560.5 1.7 reshape.255
  562.2 2.4 copy.104
  564.6 1.8 reshape.256
  566.4 2.8 collective-permute-start.17
  569.2 2.5 collective-permute-start.16
  571.7 4.2 collective-permute-start.15
  575.9 1.9 collective-permute-start.14
  577.8 4.0 collective-permute-start.13
  581.8 9.7 %fusion.3 = bf16[256,1536]{1,0:T(8,128)(2,1)S(1)} fusion(f32[256,1536]{1,0:T(8,128)S(1)} %bitcast.68, bf16[1536,4608]{1,0:T(8,128)(2,1)} %param.8, bf16[256,1536]{1,0:T(8,128)(2,1)} %reshape.257, bf16[256,1536]{1,0:T(8,128)(2,1)} %reshape.256, bf16[256,1536]{1,0:T(8,128)(2,1)} %reshape.255), kind=kOutput, calls=%fused_computation.12 | convolution fusion | flops 3631742976 | bytes 18874368 | tf_op jit(solution)/shard_map/dot_general | solution.py:150
  593.4 2.8 collective-permute-start.11
  596.1 4.7 collective-permute-start.10
  600.8 2.1 collective-permute-start.9
  603.0 2.5 collective-permute-start.8
  605.4 2.8 fusion.2
  612.1 51.7 %concatenate.37 = f32[524,1536]{1,0:T(8,128)} concatenate(f32[12,1536]{1,0:T(8,128)S(1)} %copy-done.15, f32[16,1536]{1,0:T(8,128)} %collective-permute-done.38, f32[16,1536]{1,0:T(8,128)} %collective-permute-done.37, f32[16,1536]{1,0:T(8,128)} %collective-permute-done.36, f32[16,1536]{1,0:T(8,128)} %collective-permute-done.35, f32[16,1536]{1,0:T(8,128)S(1)} %collective-permute-done.34, ...), dimensions={0} | concatenate | bytes 6438912
  665.4 63.3 %all-reduce.2 = (f32[]{:T(128)}, f32[24,225]{1,0:T(8,128)S(1)}, f32[1536]{0:T(1024)S(1)}, f32[1536]{0:T(1024)S(1)}) all-reduce(f32[]{:T(128)} %multiply_reduce_fusion.4, f32[24,225]{1,0:T(8,128)S(1)} %copy-done.45, f32[1536]{0:T(1024)S(1)} %get-tuple-element.30, f32[1536]{0:T(1024)S(1)} %fusion.34), channel_id=1, replica_groups=mesh['lon'=32,'lat'=4] {'lon','lat'}, use_global_device_ids=true, to_apply=%region_9.10 | all-reduce | flops 8473 | bytes 67784 | tf_op jit(solution)/shard_map/psum | solution.py:165
  737.0 4.9 collective-permute-start.3
  742.0 9.0 %collective-permute-start.7 = (bf16[16,4,1536]{2,1,0:T(4,128)(2,1)S(1)}, bf16[16,4,1536]{2,1,0:T(4,128)(2,1)S(1)}, u32[]{:S(2)}, u32[]{:S(2)}) collective-permute-start(bf16[16,4,1536]{2,1,0:T(4,128)(2,1)S(1)} %pad_maximum_fusion.3), channel_id=1, source_target_pairs={{0,4},{4,8},{8,12},{12,16},{16,20},{20,24},{24,28},{28,32},{32,36}... | collective-permute-start | bytes 589832 | tf_op jit(solution)/shard_map/ppermute | solution.py:17
  751.0 3.6 collective-permute-done.3
  755.7 7.9 %collective-permute-done.7 = bf16[16,4,1536]{2,1,0:T(4,128)(2,1)S(1)} collective-permute-done((bf16[16,4,1536]{2,1,0:T(4,128)(2,1)S(1)}, bf16[16,4,1536]{2,1,0:T(4,128)(2,1)S(1)}, u32[]{:S(2)}, u32[]{:S(2)}) %collective-permute-start.7) | collective-permute-done | bytes 196640 | tf_op jit(solution)/shard_map/ppermute | solution.py:17
  (201 shorter events, 39.9 us)
Async XLA Ops:
  0.6 22.8 %copy-start.12 = (bf16[16,16,1536]{2,1,0:T(8,128)(2,1)S(1)}, bf16[16,16,1536]{2,1,0:T(8,128)(2,1)}, u32[]{:S(2)}) copy-start(bf16[16,16,1536]{2,1,0:T(8,128)(2,1)} %param.13) | copy-start | bytes 2359300
  1.8 28.7 %collective-permute-start.4 = (bf16[16,4,1536]{2,1,0:T(4,128)(2,1)S(1)}, bf16[16,4,1536]{2,1,0:T(4,128)(2,1)S(1)}, u32[]{:S(2)}, u32[]{:S(2)}) collective-permute-start(bf16[16,4,1536]{2,1,0:T(4,128)(2,1)S(1)} %slice.69), channel_id=1, source_target_pairs={{0,124},{4,0},{8,4},{12,8},{16,12},{20,16},{24,20},{28,24},{32,28}... | collective-permute-start | bytes 589832 | tf_op jit(solution)/shard_map/ppermute | solution.py:17
  13.1 16.4 %collective-permute-start = (bf16[16,4,1536]{2,1,0:T(4,128)(2,1)S(1)}, bf16[16,4,1536]{2,1,0:T(4,128)(2,1)S(1)}, u32[]{:S(2)}, u32[]{:S(2)}) collective-permute-start(bf16[16,4,1536]{2,1,0:T(4,128)(2,1)S(1)} %slice.58), channel_id=1, source_target_pairs={{0,124},{4,0},{8,4},{12,8},{16,12},{20,16},{24,20},{28,24},{32,28}... | collective-permute-start | bytes 589832 | tf_op jit(solution)/shard_map/ppermute | solution.py:17
  29.5 10.9 %collective-permute-start.1 = (bf16[4,16,1536]{2,1,0:T(8,128)(2,1)S(1)}, bf16[4,16,1536]{2,1,0:T(8,128)(2,1)S(1)}, u32[]{:S(2)}, u32[]{:S(2)}) collective-permute-start(bf16[4,16,1536]{2,1,0:T(8,128)(2,1)S(1)} %pad_maximum_fusion.6), channel_id=1, source_target_pairs={{0,3},{1,0},{2,1},{3,2},{4,7},{5,4},{6,5},{7,6},{8,11},{9,8},{10,9... | collective-permute-start | bytes 589832 | tf_op jit(solution)/shard_map/ppermute | solution.py:17
  30.5 12.7 %collective-permute-start.5 = (bf16[4,16,1536]{2,1,0:T(8,128)(2,1)S(1)}, bf16[4,16,1536]{2,1,0:T(8,128)(2,1)S(1)}, u32[]{:S(2)}, u32[]{:S(2)}) collective-permute-start(bf16[4,16,1536]{2,1,0:T(8,128)(2,1)S(1)} %pad_maximum_fusion.4), channel_id=1, source_target_pairs={{0,3},{1,0},{2,1},{3,2},{4,7},{5,4},{6,5},{7,6},{8,11},{9,8},{10,9... | collective-permute-start | bytes 589832 | tf_op jit(solution)/shard_map/ppermute | solution.py:17
  67.1 5.4 copy-start.10
  72.5 3.8 copy-start.42
  87.7 4.8 copy-start.4
  475.6 18.6 %collective-permute-start.38 = (f32[16,1536]{1,0:T(8,128)S(1)}, f32[16,1536]{1,0:T(8,128)}, u32[]{:S(2)}, u32[]{:S(2)}) collective-permute-start(f32[16,1536]{1,0:T(8,128)S(1)} %fusion), channel_id=1, source_target_pairs={{0,31},{1,32},{2,33},{3,34},{4,35},{5,36},{6,37},{7,38},{8,39},{9,... | collective-permute-start | bytes 294920
  477.5 20.1 %collective-permute-start.37 = (f32[16,1536]{1,0:T(8,128)S(1)}, f32[16,1536]{1,0:T(8,128)}, u32[]{:S(2)}, u32[]{:S(2)}) collective-permute-start(f32[16,1536]{1,0:T(8,128)S(1)} %fusion), channel_id=1, source_target_pairs={{0,30},{1,31},{2,32},{3,33},{4,34},{5,35},{6,36},{7,37},{8,38},{9,... | collective-permute-start | bytes 294920
  479.5 19.6 %collective-permute-start.36 = (f32[16,1536]{1,0:T(8,128)S(1)}, f32[16,1536]{1,0:T(8,128)}, u32[]{:S(2)}, u32[]{:S(2)}) collective-permute-start(f32[16,1536]{1,0:T(8,128)S(1)} %fusion), channel_id=1, source_target_pairs={{0,29},{1,30},{2,31},{3,32},{4,33},{5,34},{6,35},{7,36},{8,37},{9,... | collective-permute-start | bytes 294920
  481.4 32.1 %collective-permute-start.35 = (f32[16,1536]{1,0:T(8,128)S(1)}, f32[16,1536]{1,0:T(8,128)}, u32[]{:S(2)}, u32[]{:S(2)}) collective-permute-start(f32[16,1536]{1,0:T(8,128)S(1)} %fusion), channel_id=1, source_target_pairs={{0,28},{1,29},{2,30},{3,31},{4,32},{5,33},{6,34},{7,35},{8,36},{9,... | collective-permute-start | bytes 294920
  487.5 8.0 %copy-start.43 = (f32[4,24,64]{2,1,0:T(8,128)S(1)}, f32[4,24,64]{2,1,0:T(8,128)}, u32[]{:S(2)}) copy-start(f32[4,24,64]{2,1,0:T(8,128)} %copy-done.42) | copy-start | bytes 73732
  487.5 5.4 collective-permute-start.39
  488.9 6.6 copy-start.9
  492.9 4.7 copy-start.14
  492.9 22.9 %collective-permute-start.34 = (f32[16,1536]{1,0:T(8,128)S(1)}, f32[16,1536]{1,0:T(8,128)S(1)}, u32[]{:S(2)}, u32[]{:S(2)}) collective-permute-start(f32[16,1536]{1,0:T(8,128)S(1)} %fusion), channel_id=1, source_target_pairs={{0,27},{1,28},{2,29},{3,30},{4,31},{5,32},{6,33},{7,34},{8,35},{9,... | collective-permute-start | bytes 294920
  494.2 27.0 %collective-permute-start.33 = (f32[16,1536]{1,0:T(8,128)S(1)}, f32[16,1536]{1,0:T(8,128)S(1)}, u32[]{:S(2)}, u32[]{:S(2)}) collective-permute-start(f32[16,1536]{1,0:T(8,128)S(1)} %fusion), channel_id=1, source_target_pairs={{0,26},{1,27},{2,28},{3,29},{4,30},{5,31},{6,32},{7,33},{8,34},{9,... | collective-permute-start | bytes 294920
  495.5 27.0 %copy-start.11 = (bf16[4,64,24,64]{1,3,2,0:T(8,128)(2,1)S(1)}, bf16[4,64,24,64]{1,3,2,0:T(8,128)(2,1)}, u32[]{:S(2)}) copy-start(bf16[4,64,24,64]{1,3,2,0:T(8,128)(2,1)} %copy.105) | copy-start | bytes 2359300
  497.6 36.8 %copy-start.1 = (bf16[4,64,24,64]{1,3,2,0:T(8,128)(2,1)S(1)}, bf16[4,64,24,64]{1,3,2,0:T(8,128)(2,1)}, u32[]{:S(2)}) copy-start(bf16[4,64,24,64]{1,3,2,0:T(8,128)(2,1)} %copy.101) | copy-start | bytes 2359300
  497.6 27.1 %collective-permute-start.32 = (f32[16,1536]{1,0:T(8,128)S(1)}, f32[16,1536]{1,0:T(8,128)S(1)}, u32[]{:S(2)}, u32[]{:S(2)}) collective-permute-start(f32[16,1536]{1,0:T(8,128)S(1)} %fusion), channel_id=1, source_target_pairs={{0,25},{1,26},{2,27},{3,28},{4,29},{5,30},{6,31},{7,32},{8,33},{9,... | collective-permute-start | bytes 294920
  499.1 26.9 %collective-permute-start.31 = (f32[16,1536]{1,0:T(8,128)S(1)}, f32[16,1536]{1,0:T(8,128)S(1)}, u32[]{:S(2)}, u32[]{:S(2)}) collective-permute-start(f32[16,1536]{1,0:T(8,128)S(1)} %fusion), channel_id=1, source_target_pairs={{0,24},{1,25},{2,26},{3,27},{4,28},{5,29},{6,30},{7,31},{8,32},{9,... | collective-permute-start | bytes 294920
  513.5 14.2 %collective-permute-start.30 = (f32[16,1536]{1,0:T(8,128)S(1)}, f32[16,1536]{1,0:T(8,128)S(1)}, u32[]{:S(2)}, u32[]{:S(2)}) collective-permute-start(f32[16,1536]{1,0:T(8,128)S(1)} %fusion), channel_id=1, source_target_pairs={{0,23},{1,24},{2,25},{3,26},{4,27},{5,28},{6,29},{7,30},{8,31},{9,... | collective-permute-start | bytes 294920
  515.8 13.6 %collective-permute-start.29 = (f32[16,1536]{1,0:T(8,128)S(1)}, f32[16,1536]{1,0:T(8,128)S(1)}, u32[]{:S(2)}, u32[]{:S(2)}) collective-permute-start(f32[16,1536]{1,0:T(8,128)S(1)} %fusion), channel_id=1, source_target_pairs={{0,22},{1,23},{2,24},{3,25},{4,26},{5,27},{6,28},{7,29},{8,30},{9,... | collective-permute-start | bytes 294920
  521.2 9.5 %collective-permute-start.28 = (f32[16,1536]{1,0:T(8,128)S(1)}, f32[16,1536]{1,0:T(8,128)S(1)}, u32[]{:S(2)}, u32[]{:S(2)}) collective-permute-start(f32[16,1536]{1,0:T(8,128)S(1)} %fusion), channel_id=1, source_target_pairs={{0,21},{1,22},{2,23},{3,24},{4,25},{5,26},{6,27},{7,28},{8,29},{9,... | collective-permute-start | bytes 294920
  524.7 11.9 %copy-start.18 = (f32[16,1536]{1,0:T(8,128)}, f32[16,1536]{1,0:T(8,128)S(1)}, u32[]{:S(2)}) copy-start(f32[16,1536]{1,0:T(8,128)S(1)} %collective-permute-done.32) | copy-start | bytes 294916
  524.7 11.9 %collective-permute-start.27 = (f32[16,1536]{1,0:T(8,128)S(1)}, f32[16,1536]{1,0:T(8,128)S(1)}, u32[]{:S(2)}, u32[]{:S(2)}) collective-permute-start(f32[16,1536]{1,0:T(8,128)S(1)} %fusion), channel_id=1, source_target_pairs={{0,20},{1,21},{2,22},{3,23},{4,24},{5,25},{6,26},{7,27},{8,28},{9,... | collective-permute-start | bytes 294920
  526.0 10.6 %copy-start.20 = (f32[16,1536]{1,0:T(8,128)}, f32[16,1536]{1,0:T(8,128)S(1)}, u32[]{:S(2)}) copy-start(f32[16,1536]{1,0:T(8,128)S(1)} %collective-permute-done.31) | copy-start | bytes 294916
  526.0 16.2 %collective-permute-start.26 = (f32[16,1536]{1,0:T(8,128)S(1)}, f32[16,1536]{1,0:T(8,128)S(1)}, u32[]{:S(2)}, u32[]{:S(2)}) collective-permute-start(f32[16,1536]{1,0:T(8,128)S(1)} %fusion), channel_id=1, source_target_pairs={{0,19},{1,20},{2,21},{3,22},{4,23},{5,24},{6,25},{7,26},{8,27},{9,... | collective-permute-start | bytes 294920
  527.7 8.9 %copy-start.22 = (f32[16,1536]{1,0:T(8,128)}, f32[16,1536]{1,0:T(8,128)S(1)}, u32[]{:S(2)}) copy-start(f32[16,1536]{1,0:T(8,128)S(1)} %collective-permute-done.30) | copy-start | bytes 294916
  527.7 16.5 %collective-permute-start.25 = (f32[16,1536]{1,0:T(8,128)S(1)}, f32[16,1536]{1,0:T(8,128)S(1)}, u32[]{:S(2)}, u32[]{:S(2)}) collective-permute-start(f32[16,1536]{1,0:T(8,128)S(1)} %fusion), channel_id=1, source_target_pairs={{0,18},{1,19},{2,20},{3,21},{4,22},{5,23},{6,24},{7,25},{8,26},{9,... | collective-permute-start | bytes 294920
  529.4 7.1 copy-start.24
  529.4 17.0 %collective-permute-start.24 = (f32[16,1536]{1,0:T(8,128)S(1)}, f32[16,1536]{1,0:T(8,128)S(1)}, u32[]{:S(2)}, u32[]{:S(2)}) collective-permute-start(f32[16,1536]{1,0:T(8,128)S(1)} %fusion), channel_id=1, source_target_pairs={{0,17},{1,18},{2,19},{3,20},{4,21},{5,22},{6,23},{7,24},{8,25},{9,... | collective-permute-start | bytes 294920
  530.7 5.8 copy-start.26
  530.8 17.9 %collective-permute-start.23 = (f32[16,1536]{1,0:T(8,128)S(1)}, f32[16,1536]{1,0:T(8,128)S(1)}, u32[]{:S(2)}, u32[]{:S(2)}) collective-permute-start(f32[16,1536]{1,0:T(8,128)S(1)} %fusion), channel_id=1, source_target_pairs={{0,16},{1,17},{2,18},{3,19},{4,20},{5,21},{6,22},{7,23},{8,24},{9,... | collective-permute-start | bytes 294920
  534.4 17.6 %copy-start = (bf16[4,64,24,64]{1,3,2,0:T(8,128)(2,1)S(1)}, bf16[4,64,24,64]{1,3,2,0:T(8,128)(2,1)}, u32[]{:S(2)}) copy-start(bf16[4,64,24,64]{1,3,2,0:T(8,128)(2,1)} %copy.97) | copy-start | bytes 2359300
  536.6 15.4 %copy-start.28 = (f32[16,1536]{1,0:T(8,128)}, f32[16,1536]{1,0:T(8,128)S(1)}, u32[]{:S(2)}) copy-start(f32[16,1536]{1,0:T(8,128)S(1)} %collective-permute-done.27) | copy-start | bytes 294916
  536.6 29.8 %collective-permute-start.22 = (f32[16,1536]{1,0:T(8,128)S(1)}, f32[16,1536]{1,0:T(8,128)}, u32[]{:S(2)}, u32[]{:S(2)}) collective-permute-start(f32[16,1536]{1,0:T(8,128)S(1)} %fusion), channel_id=1, source_target_pairs={{0,15},{1,16},{2,17},{3,18},{4,19},{5,20},{6,21},{7,22},{8,23},{9,... | collective-permute-start | bytes 294920
  542.2 9.7 %copy-start.30 = (f32[16,1536]{1,0:T(8,128)}, f32[16,1536]{1,0:T(8,128)S(1)}, u32[]{:S(2)}) copy-start(f32[16,1536]{1,0:T(8,128)S(1)} %collective-permute-done.26) | copy-start | bytes 294916
  542.2 27.0 %collective-permute-start.21 = (f32[16,1536]{1,0:T(8,128)S(1)}, f32[16,1536]{1,0:T(8,128)}, u32[]{:S(2)}, u32[]{:S(2)}) collective-permute-start(f32[16,1536]{1,0:T(8,128)S(1)} %fusion), channel_id=1, source_target_pairs={{0,14},{1,15},{2,16},{3,17},{4,18},{5,19},{6,20},{7,21},{8,22},{9,... | collective-permute-start | bytes 294920
  544.2 7.8 %copy-start.32 = (f32[16,1536]{1,0:T(8,128)}, f32[16,1536]{1,0:T(8,128)S(1)}, u32[]{:S(2)}) copy-start(f32[16,1536]{1,0:T(8,128)S(1)} %collective-permute-done.25) | copy-start | bytes 294916
  544.2 27.6 %collective-permute-start.20 = (f32[16,1536]{1,0:T(8,128)S(1)}, f32[16,1536]{1,0:T(8,128)}, u32[]{:S(2)}, u32[]{:S(2)}) collective-permute-start(f32[16,1536]{1,0:T(8,128)S(1)} %fusion), channel_id=1, source_target_pairs={{0,13},{1,14},{2,15},{3,16},{4,17},{5,18},{6,19},{7,20},{8,21},{9,... | collective-permute-start | bytes 294920
  546.4 5.5 copy-start.34
  546.4 29.5 %collective-permute-start.19 = (f32[16,1536]{1,0:T(8,128)S(1)}, f32[16,1536]{1,0:T(8,128)}, u32[]{:S(2)}, u32[]{:S(2)}) collective-permute-start(f32[16,1536]{1,0:T(8,128)S(1)} %fusion), channel_id=1, source_target_pairs={{0,12},{1,13},{2,14},{3,15},{4,16},{5,17},{6,18},{7,19},{8,20},{9,... | collective-permute-start | bytes 294920
  548.6 29.2 %collective-permute-start.18 = (f32[16,1536]{1,0:T(8,128)S(1)}, f32[16,1536]{1,0:T(8,128)}, u32[]{:S(2)}, u32[]{:S(2)}) collective-permute-start(f32[16,1536]{1,0:T(8,128)S(1)} %fusion), channel_id=1, source_target_pairs={{0,11},{1,12},{2,13},{3,14},{4,15},{5,16},{6,17},{7,18},{8,19},{9,... | collective-permute-start | bytes 294920
  566.4 25.7 %collective-permute-start.17 = (f32[16,1536]{1,0:T(8,128)S(1)}, f32[16,1536]{1,0:T(8,128)}, u32[]{:S(2)}, u32[]{:S(2)}) collective-permute-start(f32[16,1536]{1,0:T(8,128)S(1)} %fusion), channel_id=1, source_target_pairs={{0,10},{1,11},{2,12},{3,13},{4,14},{5,15},{6,16},{7,17},{8,18},{9,... | collective-permute-start | bytes 294920
  569.2 24.1 %collective-permute-start.16 = (f32[16,1536]{1,0:T(8,128)S(1)}, f32[16,1536]{1,0:T(8,128)}, u32[]{:S(2)}, u32[]{:S(2)}) collective-permute-start(f32[16,1536]{1,0:T(8,128)S(1)} %fusion), channel_id=1, source_target_pairs={{0,9},{1,10},{2,11},{3,12},{4,13},{5,14},{6,15},{7,16},{8,17},{9,1... | collective-permute-start | bytes 294920
  571.7 24.4 %collective-permute-start.15 = (f32[16,1536]{1,0:T(8,128)S(1)}, f32[16,1536]{1,0:T(8,128)}, u32[]{:S(2)}, u32[]{:S(2)}) collective-permute-start(f32[16,1536]{1,0:T(8,128)S(1)} %fusion), channel_id=1, source_target_pairs={{0,8},{1,9},{2,10},{3,11},{4,12},{5,13},{6,14},{7,15},{8,16},{9,17... | collective-permute-start | bytes 294920
  575.9 24.9 %collective-permute-start.14 = (f32[16,1536]{1,0:T(8,128)S(1)}, f32[16,1536]{1,0:T(8,128)}, u32[]{:S(2)}, u32[]{:S(2)}) collective-permute-start(f32[16,1536]{1,0:T(8,128)S(1)} %fusion), channel_id=1, source_target_pairs={{0,7},{1,8},{2,9},{3,10},{4,11},{5,12},{6,13},{7,14},{8,15},{9,16}... | collective-permute-start | bytes 294920
  577.8 25.2 %collective-permute-start.13 = (f32[16,1536]{1,0:T(8,128)S(1)}, f32[16,1536]{1,0:T(8,128)}, u32[]{:S(2)}, u32[]{:S(2)}) collective-permute-start(f32[16,1536]{1,0:T(8,128)S(1)} %fusion), channel_id=1, source_target_pairs={{0,6},{1,7},{2,8},{3,9},{4,10},{5,11},{6,12},{7,13},{8,14},{9,15},... | collective-permute-start | bytes 294920
  581.8 9.7 %copy-start.6 = (f32[24,64,64]{1,2,0:T(8,128)S(1)}, f32[24,64,64]{1,2,0:T(8,128)}, u32[]{:S(2)}) copy-start(f32[24,64,64]{1,2,0:T(8,128)} %get-tuple-element.36) | copy-start | bytes 1179652
  591.7 16.5 %copy-start.5 = (bf16[256,1536]{1,0:T(8,128)(2,1)S(1)}, bf16[256,1536]{1,0:T(8,128)(2,1)}, u32[]{:S(2)}) copy-start(bf16[256,1536]{1,0:T(8,128)(2,1)} %get-tuple-element.42) | copy-start | bytes 2359300
  592.0 17.5 %collective-permute-start.12 = (f32[16,1536]{1,0:T(8,128)S(1)}, f32[16,1536]{1,0:T(8,128)S(1)}, u32[]{:S(2)}, u32[]{:S(2)}) collective-permute-start(f32[16,1536]{1,0:T(8,128)S(1)} %fusion), channel_id=1, source_target_pairs={{0,5},{1,6},{2,7},{3,8},{4,9},{5,10},{6,11},{7,12},{8,13},{9,14},{... | collective-permute-start | bytes 294920
  593.4 16.9 %collective-permute-start.11 = (f32[16,1536]{1,0:T(8,128)S(1)}, f32[16,1536]{1,0:T(8,128)}, u32[]{:S(2)}, u32[]{:S(2)}) collective-permute-start(f32[16,1536]{1,0:T(8,128)S(1)} %fusion), channel_id=1, source_target_pairs={{0,4},{1,5},{2,6},{3,7},{4,8},{5,9},{6,10},{7,11},{8,12},{9,13},{1... | collective-permute-start | bytes 294920
  596.1 14.6 %collective-permute-start.10 = (f32[16,1536]{1,0:T(8,128)S(1)}, f32[16,1536]{1,0:T(8,128)S(1)}, u32[]{:S(2)}, u32[]{:S(2)}) collective-permute-start(f32[16,1536]{1,0:T(8,128)S(1)} %fusion), channel_id=1, source_target_pairs={{0,3},{1,4},{2,5},{3,6},{4,7},{5,8},{6,9},{7,10},{8,11},{9,12},{10... | collective-permute-start | bytes 294920
  600.8 9.9 %collective-permute-start.9 = (f32[16,1536]{1,0:T(8,128)S(1)}, f32[16,1536]{1,0:T(8,128)S(1)}, u32[]{:S(2)}, u32[]{:S(2)}) collective-permute-start(f32[16,1536]{1,0:T(8,128)S(1)} %fusion), channel_id=1, source_target_pairs={{0,2},{1,3},{2,4},{3,5},{4,6},{5,7},{6,8},{7,9},{8,10},{9,11},{10,... | collective-permute-start | bytes 294920
  603.0 9.0 %collective-permute-start.8 = (f32[16,1536]{1,0:T(8,128)S(1)}, f32[16,1536]{1,0:T(8,128)}, u32[]{:S(2)}, u32[]{:S(2)}) collective-permute-start(f32[16,1536]{1,0:T(8,128)S(1)} %fusion), channel_id=1, source_target_pairs={{0,1},{1,2},{2,3},{3,4},{4,5},{5,6},{6,7},{7,8},{8,9},{9,10},{10,1... | collective-permute-start | bytes 294920
  608.5 3.5 copy-start.15
  608.5 3.5 copy-start.17
  609.6 55.8 %copy-start.45 = (f32[24,225]{1,0:T(8,128)S(1)}, f32[24,225]{1,0:T(8,128)}, u32[]{:S(2)}) copy-start(f32[24,225]{1,0:T(8,128)} %fusion.2) | copy-start | bytes 64804
  609.6 127.3 %collective-permute-start.2 = (bf16[4,16,1536]{2,1,0:T(8,128)(2,1)S(1)}, bf16[4,16,1536]{2,1,0:T(8,128)(2,1)S(1)}, u32[]{:S(2)}, u32[]{:S(2)}) collective-permute-start(bf16[4,16,1536]{2,1,0:T(8,128)(2,1)S(1)} %slice.81), channel_id=1, source_target_pairs={{0,1},{1,2},{2,3},{3,0},{4,5},{5,6},{6,7},{7,4},{8,9},{9,10},{10,1... | collective-permute-start | bytes 589832 | tf_op jit(solution)/shard_map/ppermute | solution.py:17
  610.2 131.7 %collective-permute-start.6 = (bf16[4,16,1536]{2,1,0:T(8,128)(2,1)S(1)}, bf16[4,16,1536]{2,1,0:T(8,128)(2,1)S(1)}, u32[]{:S(2)}, u32[]{:S(2)}) collective-permute-start(bf16[4,16,1536]{2,1,0:T(8,128)(2,1)S(1)} %slice.85), channel_id=1, source_target_pairs={{0,1},{1,2},{2,3},{3,0},{4,5},{5,6},{6,7},{7,4},{8,9},{9,10},{10,1... | collective-permute-start | bytes 589832 | tf_op jit(solution)/shard_map/ppermute | solution.py:17
  737.0 17.6 %collective-permute-start.3 = (bf16[16,4,1536]{2,1,0:T(4,128)(2,1)S(1)}, bf16[16,4,1536]{2,1,0:T(4,128)(2,1)S(1)}, u32[]{:S(2)}, u32[]{:S(2)}) collective-permute-start(bf16[16,4,1536]{2,1,0:T(4,128)(2,1)S(1)} %pad_maximum_fusion.5), channel_id=1, source_target_pairs={{0,4},{4,8},{8,12},{12,16},{16,20},{20,24},{24,28},{28,32},{32,36}... | collective-permute-start | bytes 589832 | tf_op jit(solution)/shard_map/ppermute | solution.py:17
  742.0 21.6 %collective-permute-start.7 = (bf16[16,4,1536]{2,1,0:T(4,128)(2,1)S(1)}, bf16[16,4,1536]{2,1,0:T(4,128)(2,1)S(1)}, u32[]{:S(2)}, u32[]{:S(2)}) collective-permute-start(bf16[16,4,1536]{2,1,0:T(4,128)(2,1)S(1)} %pad_maximum_fusion.3), channel_id=1, source_target_pairs={{0,4},{4,8},{8,12},{12,16},{16,20},{20,24},{24,28},{28,32},{32,36}... | collective-permute-start | bytes 589832 | tf_op jit(solution)/shard_map/ppermute | solution.py:17
  (24 other events, 57.6 us)
where the time goes:
time: 772 us; the launch traced here: 765 us
  blocking collectives  441 us (57%)
  starting transfers between devices  135 us (17%)
  local copies, waits for them, and re-layouts  98.1 us (13%)
  matrix products  57.8 us (7%)
  other arithmetic  15.1 us (2%)
  waiting for transfers between devices  13.4 us (2%)
    unnamed x1, blocking collectives  378 us
    unnamed x32, starting transfers between devices  90.2 us
    psum x1, blocking collectives, on_device(): spread_squares = lax.psum(shard_squares, ('lon', 'lat'))  63.3 us
    unnamed x99, local copies, waits for them, and re-layouts  57 us
    ppermute x8, starting transfers between devices, from_behind(): return lax.ppermute(value, axis, pairs)  44.6 us
    reshape x7, local copies, waits for them, and re-layouts, split_heads(): return flat_rows.reshape(windows, window_cells, head_count, head_size)  15.8 us
  transfers between devices with their start and end apart: 40, of which 3 were waited for; matrix products, arithmetic and copies ran while one was open for 15% of the time, Pallas kernels for 0%

commit v1 on v0

v1 whole, which is shorter than its diff:
```python
import functools

import jax
import jax.numpy as jnp
from jax import lax
from jax.experimental import pallas as pl
from jax.experimental.pallas import tpu as pltpu
from jax.sharding import PartitionSpec as P

F32 = jnp.float32
BF = jnp.bfloat16
MESH = pl.DeviceIdType.MESH

D = 1536
HEADS = 24
GROUPS = 6
LANES = 256
TOKENS = 256
CELLS = 64
WINDOWS = 4
HALF = 768
PARAMS = 2367768
norm_epsilon = 1e-05
clip_epsilon = 1e-06

ORDERS = (("x", "y", "z"), ("y", "z", "x"), ("z", "x", "y"))


def dot(a, b, ca, cb):
    return lax.dot_general(a, b, (((ca,), (cb,)), ((), ())), preferred_element_type=F32)


def dot_exact(a, b, cb):
    total = None
    for _ in range(3):
        part = a.astype(BF)
        a = a - part.astype(F32)
        term = dot(part, b, 1, cb)
        total = term if total is None else total + term
    return total


def stack(*pieces):
    return jnp.concatenate(pieces, axis=0)


def turn(value):
    return pltpu.roll(value, 4, 0)


def low_rows(columns):
    return lax.broadcasted_iota(jnp.int32, (8, columns), 0) < 4


def halves(ref, rows, cols):
    both = ref[rows, cols].astype(F32)
    return both[:8], both[8:]


def row_halves(block, row, cols):
    both = block[row, :, cols].astype(F32)
    return both[:8], both[8:]


def columns_of(step, width=LANES):
    return pl.ds(pl.multiple_of(step * width, width), width)


def input_strips(block, strips, cols, low):
    for k in range(3):
        a, b, c, d = [row_halves(block, 4 + 4 * k + i, cols)[0] for i in range(4)]
        strips[16 * k : 16 * k + 16, cols] = stack(
            jnp.where(low, a, turn(b)), jnp.where(low, c, turn(d))
        ).astype(BF)
    t = [row_halves(block, r, cols) for r in range(4)]
    wide = [turn(jnp.where(low, t1, t0)) for t0, t1 in t]
    strips[48:64, cols] = stack(wide[0], wide[1]).astype(BF)
    strips[64:80, cols] = stack(wide[2], wide[3]).astype(BF)
    strips[80:96, cols] = stack(
        jnp.where(low, turn(t[0][1]), t[1][1]), jnp.where(low, turn(t[2][1]), t[3][1])
    ).astype(BF)
    strips[96:112, cols] = stack(
        jnp.where(low, t[0][0], turn(t[1][0])), jnp.where(low, t[2][0], turn(t[3][0]))
    ).astype(BF)


def input_windows(block, came, flat, cols, low):
    for k in range(3):
        pairs = halves(came, slice(16 * k, 16 * k + 16), cols)
        for i in range(2):
            r = 4 * k + 2 * i
            s = pairs[i]
            at = (r // 8) * 128 + (r % 8) * 8
            t0, t1 = row_halves(block, r + 4, cols)
            u0, u1 = row_halves(block, r + 5, cols)
            flat[at : at + 16, cols] = stack(
                turn(jnp.where(low, t1, t0)), turn(jnp.where(low, u1, u0))
            ).astype(BF)
            flat[at + 64 : at + 80, cols] = stack(
                jnp.where(low, turn(t1), turn(s)), jnp.where(low, turn(u1), s)
            ).astype(BF)
    side = halves(came, slice(80, 96), cols)
    corner = halves(came, slice(96, 112), cols)
    for i in range(2):
        at = 128 + 32 + 16 * i
        flat[at : at + 16, cols] = came[48 + 16 * i : 64 + 16 * i, cols]
        s, d = side[i], corner[i]
        flat[at + 64 : at + 80, cols] = stack(
            jnp.where(low, s, turn(d)), jnp.where(low, turn(s), d)
        ).astype(BF)


def output_strips(flat, strips, cols, low):
    for k in range(3):
        parts = []
        for i in range(4):
            r = 4 * k + i
            at = (r // 8) * 128 + 64 + (r % 8) * 8
            parts.append(flat[at : at + 8, cols])
        a, b, c, d = parts
        strips[16 * k : 16 * k + 16, cols] = stack(
            jnp.where(low, turn(a), b), jnp.where(low, turn(c), d)
        ).astype(BF)
    strips[48:80, cols] = flat[160:192, cols].astype(BF)
    a, b, c, d = [flat[224 + 8 * i : 232 + 8 * i, cols] for i in range(4)]
    strips[80:96, cols] = stack(
        jnp.where(low, a, turn(b)), jnp.where(low, c, turn(d))
    ).astype(BF)
    strips[96:112, cols] = stack(
        jnp.where(low, turn(a), b), jnp.where(low, turn(c), d)
    ).astype(BF)


def output_block(flat, came, block, cols, low):
    for k in range(3):
        pairs = halves(came, slice(16 * k, 16 * k + 16), cols)
        for i in range(4):
            r = 4 * k + i
            s = pairs[i // 2]
            s = s if i % 2 == 0 else turn(s)
            at = (r // 8) * 128 + (r % 8) * 8
            a = turn(flat[at : at + 8, cols])
            b = turn(flat[at + 64 : at + 72, cols])
            block[r + 4, :, cols] = stack(jnp.where(low, s, a), jnp.where(low, a, b)).astype(BF)
    side = halves(came, slice(80, 96), cols)
    corner = halves(came, slice(96, 112), cols)
    for i in range(2):
        wides = halves(came, slice(48 + 16 * i, 64 + 16 * i), cols)
        s, d = side[i], corner[i]
        for k in range(2):
            wide = turn(wides[k])
            at_low = d if k == 0 else turn(d)
            at_high = turn(s) if k == 0 else s
            block[2 * i + k, :, cols] = stack(
                jnp.where(low, at_low, wide), jnp.where(low, wide, at_high)
            ).astype(BF)


def block_diagonal(value, lane_head):
    zero = jnp.zeros_like(value)
    return stack(*[jnp.where(lane_head == h, value, zero) for h in range(4)])


def diagonal(product, left):
    tiles = []
    for t in range(2):
        cols = slice(128 * t, 128 * t + 128)
        tiles.append(
            jnp.where(
                left,
                product[128 * t : 128 * t + 64, cols],
                product[128 * t + 64 : 128 * t + 128, cols],
            )
        )
    return jnp.concatenate(tiles, axis=1)


def sublayer(
    tok_h, wq_h, rel_ref, pw_h, gain_ref, shift_ref, cot_h,
    out_h, dtok_h, dpw_ref, drel_ref, dgain_ref, dshift_ref,
    tok_v, cot_v, w_v, pw_v, x_v, c_v, qkv_v, pt_v, mix_v, mixt_v, proj_v, flat_v,
    dp_v, dps_v, dmix_v, dqkv_v, oblk_v, dblk_v,
    e_v, wb_v, bt_v, mask_v, u_v, acc_v,
    send_x, came_x, send_c, came_c, send_o, came_o, send_d, came_d,
    p_v, r1a, r1c, s2a, s2b, s2c, r2a, r2b, r2c, s3a, s3b, s3c, r3, fin_v,
    sm_v, sq_v,
    load_sem, w_sem, store_sem, halo_send, halo_recv, mix_send, mix_recv, dp_sem,
    rs_send, rs_recv, sm_send, sm_recv, sq_send, sq_recv, fin_sem,
):
    lon = lax.axis_index("lon")
    lat = lax.axis_index("lat")
    core = lax.rem(lat, 2)
    at = {
        "x": lax.rem(lon // 4, 4),
        "y": lax.rem(lon, 4),
        "z": (lon // 16) * 2 + lat // 2,
    }

    def device(chip, on_core):
        z = chip["z"]
        return {
            "lon": (z // 2) * 16 + chip["x"] * 4 + chip["y"],
            "lat": lax.rem(z, 2) * 2 + on_core,
        }

    def along(axis, steps):
        chip = dict(at)
        chip[axis] = lax.rem(at[axis] + steps, 4)
        return device(chip, core)

    sibling = device(at, 1 - core)

    def shifted(lat_steps, lon_steps):
        return {
            "lon": lax.rem(lon + lon_steps + 32, 32),
            "lat": lax.rem(lat + lat_steps + 4, 4),
        }

    def remote(src, dst, send, recv, target):
        return pltpu.make_async_remote_copy(
            src_ref=src, dst_ref=dst, send_sem=send, recv_sem=recv,
            device_id=target, device_id_type=MESH,
        )

    load_tok = pltpu.make_async_copy(tok_h, tok_v, load_sem.at[0])
    load_cot = pltpu.make_async_copy(cot_h, cot_v, load_sem.at[1])
    load_pw = pltpu.make_async_copy(pw_h, pw_v, load_sem.at[2])

    def load_w(chunk):
        cols = columns_of(chunk)
        return pltpu.make_async_copy(wq_h.at[:, cols], w_v.at[:, cols], w_sem.at[chunk])

    load_tok.start()
    load_cot.start()

    partners = [shifted(0, 1), shifted(0, -1), shifted(1, 0), shifted(-1, 0), shifted(1, 1), shifted(-1, -1)]
    partners += [along(axis, steps) for axis in "xyz" for steps in (1, 2, 3)] + [sibling]
    barrier = pltpu.get_barrier_semaphore()
    for partner in partners:
        pl.semaphore_signal(barrier, inc=1, device_id=partner, device_id_type=MESH)

    for g in range(GROUPS):
        for part in range(3):
            load_w(part * GROUPS + g).start()
    load_pw.start()

    low = low_rows(LANES)

    def each_column(body):
        lax.fori_loop(0, GROUPS, lambda n, _: (body(columns_of(n)), 0)[1], 0)

    def halo(strips, came, which, sign):
        rows = (slice(0, 48), slice(48, 96), slice(96, 112))
        targets = (shifted(0, sign), shifted(sign, 0), shifted(sign, sign))
        return [
            remote(
                strips.at[rows[i]], came.at[rows[i]],
                halo_send.at[which, i], halo_recv.at[which, i], targets[i],
            )
            for i in range(3)
        ]

    load_tok.wait()
    each_column(lambda cols: input_strips(tok_v, send_x, cols, low))
    pl.semaphore_wait(barrier, len(partners))
    halo_x = halo(send_x, came_x, 0, -1)
    for copy in halo_x:
        copy.start()
    load_cot.wait()
    each_column(lambda cols: input_strips(cot_v, send_c, cols, low))
    halo_c = halo(send_c, came_c, 1, -1)
    for copy in halo_c:
        copy.start()

    spot = lax.broadcasted_iota(jnp.int32, (128, LANES), 0)
    slot = lax.broadcasted_iota(jnp.int32, (128, LANES), 1)
    for cj in range(8):
        hit = ((spot >> 3) == (slot >> 4)) & ((spot & 7) - cj + 7 == (slot & 15))
        e_v[128 * cj : 128 * cj + 128, :] = jnp.where(hit, 1.0, 0.0).astype(BF)
    rel = rel_ref[...]
    for cj in range(8):
        wb_v[:, cj, :] = dot_exact(rel, e_v[128 * cj : 128 * cj + 128, :], 1)
    left8 = lax.broadcasted_iota(jnp.int32, (8, 128), 1) < 64

    def bias_step(g, _):
        for t in range(2):
            first = wb_v[g * 4 + 2 * t]
            second = wb_v[g * 4 + 2 * t + 1]
            for rj in range(8):
                shift = (7 - rj) * 8
                bt_v[g, 8 * rj : 8 * rj + 8, 128 * t : 128 * t + 128] = jnp.where(
                    left8,
                    pltpu.roll(first, (128 - shift) % 128, 1),
                    pltpu.roll(second, (192 - shift) % 128, 1),
                )
        return 0

    lax.fori_loop(0, GROUPS, bias_step, 0)
    j_upper = lax.broadcasted_iota(jnp.int32, (CELLS, LANES), 0) < 32
    i_upper = (lax.broadcasted_iota(jnp.int32, (CELLS, LANES), 1) & 63) < 32
    crossing = (j_upper != i_upper) & (lat == 3)
    mask_v[...] = jnp.where(crossing, -jnp.inf, 0.0)

    for copy in halo_x:
        copy.wait()
    each_column(lambda cols: input_windows(tok_v, came_x, x_v, cols, low))

    def qkv_step(g, _):
        for part in range(3):
            chunk = part * GROUPS + g
            load_w(chunk).wait()
            value = dot(x_v[...], w_v[:, columns_of(chunk)], 1, 0).astype(BF)
            if part == 0:
                value = value * jnp.asarray(0.125, BF)
            qkv_v[chunk] = value
        return 0

    lax.fori_loop(0, GROUPS, qkv_step, 0)

    lane_head = lax.broadcasted_iota(jnp.int32, (CELLS, LANES), 1) >> 6
    left = lax.broadcasted_iota(jnp.int32, (CELLS, 128), 1) < 64

    def mix_copy(g):
        rows = columns_of(g)
        return remote(
            mixt_v.at[0, rows], mixt_v.at[1, rows], mix_send.at[g], mix_recv.at[g], sibling
        )

    def forward_step(g, _):
        for w in range(WINDOWS):
            rows = slice(CELLS * w, CELLS * w + CELLS)
            q, k, v = [qkv_v[part * GROUPS + g, rows, :] for part in range(3)]
            scores = dot(k, block_diagonal(q, lane_head), 1, 1) + bt_v[g]
            if w >= 2:
                scores = scores + mask_v[...]
            peak = jnp.max(scores, axis=0, keepdims=True)
            raised = jnp.exp(scores - peak)
            shares = raised * (1.0 / jnp.sum(raised, axis=0, keepdims=True))
            pt_v[g, w] = shares
            mixed = diagonal(dot(shares.astype(BF), v, 0, 0), left)
            mix_v[rows, columns_of(g)] = mixed.astype(BF)
        mixt_v[0, columns_of(g), :] = mix_v[:, columns_of(g)].T
        mix_copy(g).start()
        return 0

    lax.fori_loop(0, GROUPS, forward_step, 0)

    def project_step(n, _):
        cols = columns_of(n)
        proj_v[:, cols] = dot(mix_v[...], pw_v[:, cols], 1, 0)
        return 0

    load_pw.wait()
    lax.fori_loop(0, GROUPS, project_step, 0)

    for copy in halo_c:
        copy.wait()
    each_column(lambda cols: input_windows(cot_v, came_c, c_v, cols, low))

    acc_v[...] = jnp.zeros_like(acc_v)

    def norm_step(m, _):
        rows = pl.ds(pl.multiple_of(m * 16, 16), 16)
        projected = proj_v[rows, :]
        centre = projected - jnp.mean(projected, axis=1, keepdims=True)
        inverse = lax.rsqrt(jnp.mean(centre * centre, axis=1, keepdims=True) + norm_epsilon)
        normed = centre * inverse
        flat_v[rows, :] = x_v[rows, :].astype(F32) + normed * gain_ref[...] + shift_ref[...]
        upstream = c_v[rows, :].astype(F32)
        product = upstream * normed
        acc_v[0] += product[:8] + product[8:]
        acc_v[1] += upstream[:8] + upstream[8:]
        d_normed = upstream * gain_ref[...]
        inner = d_normed - jnp.mean(d_normed, axis=1, keepdims=True)
        inner = inner - normed * jnp.mean(d_normed * normed, axis=1, keepdims=True)
        dp_v[rows, :] = (inverse * inner).astype(BF)
        return 0

    lax.fori_loop(0, TOKENS // 16, norm_step, 0)

    other_half = pl.ds(pl.multiple_of((1 - core) * HALF, HALF), HALF)
    dp_copy = remote(dp_v.at[:, other_half], dps_v, dp_sem.at[0], dp_sem.at[1], sibling)
    dp_copy.start()

    each_column(lambda cols: output_strips(flat_v, send_o, cols, low))
    halo_o = halo(send_o, came_o, 2, 1)
    for copy in halo_o:
        copy.start()

    def d_mixed_step(n, _):
        dmix_v[n] = dot(dp_v[...], pw_v[columns_of(n), :], 1, 1).astype(BF)
        return 0

    lax.fori_loop(0, GROUPS, d_mixed_step, 0)

    dp_copy.wait()
    for g in range(GROUPS):
        mix_copy(g).wait()

    def slot_of(buffer, lead, axes, axis, index):
        if axis == "z":
            places = {"h": index // 2, "l": lax.rem(index, 2)}
        else:
            places = {axis: index}
        return buffer.at[lead + tuple(places.get(name, slice(None)) for name in axes)]

    stages = (
        ((p_v, (0,), "hxyl"), (p_v, (1,), "hxyl"), (p_v, (2,), "hxyl")),
        ((s2a, (), "hyl"), (s2b, (), "hxl"), (s2c, (), "xy")),
        ((s3a, (), "hl"), (s3b, (), "x"), (s3c, (), "y")),
    )
    arrivals = (
        (r1a.at[0], r1a.at[1], r1c),
        (r2a, r2b, r2c),
        (r3.at[0], r3.at[1], r3.at[2]),
    )

    def scatter_copies(stage, part):
        buffer, lead, axes = stages[stage][part]
        axis = ORDERS[part][stage]
        copies = []
        for steps in (1, 2, 3):
            index = lax.rem(at[axis] + steps, 4)
            copies.append(
                remote(
                    slot_of(buffer, lead, axes, axis, index),
                    arrivals[stage][part].at[steps - 1],
                    rs_send.at[stage, part, steps - 1],
                    rs_recv.at[stage, part, steps - 1],
                    along(axis, steps),
                )
            )
        return copies

    def scatter_start(stage, part):
        for copy in scatter_copies(stage, part):
            copy.start()

    def scatter_sum(stage, part):
        for copy in scatter_copies(stage, part):
            copy.wait()
        buffer, lead, axes = stages[stage][part]
        axis = ORDERS[part][stage]
        total = slot_of(buffer, lead, axes, axis, at[axis])[...].astype(F32)
        for steps in range(3):
            total = total + arrivals[stage][part][steps].astype(F32)
        if stage < 2:
            target = stages[stage + 1][part][0]
            target[...] = total.astype(target.dtype)
            scatter_start(stage + 1, part)
        else:
            fin_v[0, :, LANES * part : LANES * part + 128] = total[:24]
            fin_v[0, :, LANES * part + 128 : LANES * part + 256] = total[24:]

    for part in range(3):
        own = dp_v[:, pl.ds(pl.multiple_of(core * HALF + part * LANES, LANES), LANES)]
        other = dps_v[:, LANES * part : LANES * part + LANES]
        for mb in range(4):
            rows = slice(384 * mb, 384 * mb + 384)
            value = dot(mixt_v[0, rows, :], own, 1, 0) + dot(mixt_v[1, rows, :], other, 1, 0)
            value = jnp.concatenate(
                [value[:, :128].reshape(16, 24, 128), value[:, 128:].reshape(16, 24, 128)], axis=1
            )
            p_v[part, mb // 2, 2 * (mb % 2) : 2 * (mb % 2) + 2] = value.astype(BF).reshape(
                2, 4, 2, 48, 128
            )
        scatter_start(0, part)

    def backward_step(g, _):
        total = None
        for w in range(WINDOWS):
            rows = slice(CELLS * w, CELLS * w + CELLS)
            q, k, v = [qkv_v[part * GROUPS + g, rows, :] for part in range(3)]
            d_out = block_diagonal(dmix_v[g, rows, :], lane_head)
            shares = pt_v[g, w]
            d_shares = dot(v, d_out, 1, 1)
            d_scores = shares * (d_shares - jnp.sum(shares * d_shares, axis=0, keepdims=True))
            total = d_scores if total is None else total + d_scores
            low_scores = d_scores.astype(BF)
            dq = diagonal(dot(low_scores, k, 0, 0), left) * 0.125
            dk = dot(low_scores, block_diagonal(q, lane_head), 1, 0)
            dv = dot(shares.astype(BF), d_out, 1, 0)
            for part, value in enumerate((dq, dk, dv)):
                dqkv_v[rows, columns_of(part * GROUPS + g)] = value.astype(BF)
        for t in range(2):
            sums = [None, None]
            for rj in range(8):
                shift = (7 - rj) * 8
                piece = total[8 * rj : 8 * rj + 8, 128 * t : 128 * t + 128]
                pair = (
                    pltpu.roll(jnp.where(left8, piece, 0.0), shift, 1),
                    pltpu.roll(jnp.where(left8, 0.0, piece), shift + 64, 1),
                )
                sums = [b if a is None else a + b for a, b in zip(sums, pair)]
            u_v[g * 4 + 2 * t] = sums[0]
            u_v[g * 4 + 2 * t + 1] = sums[1]
        return 0

    lax.fori_loop(0, GROUPS, backward_step, 0)

    small = None
    for cj in range(8):
        term = dot_exact(u_v[:, cj, :], e_v[128 * cj : 128 * cj + 128, :], 0)
        small = term if small is None else small + term
    gain_sum = jnp.sum(acc_v[0], axis=0, keepdims=True)
    shift_sum = jnp.sum(acc_v[1], axis=0, keepdims=True)
    zero2 = jnp.zeros((2, LANES), F32)
    small = stack(
        small,
        *[gain_sum[:, LANES * n : LANES * n + LANES] for n in range(GROUPS)], zero2,
        *[shift_sum[:, LANES * n : LANES * n + LANES] for n in range(GROUPS)], zero2,
    )

    def sum_copies(buffer, send, recv, stage):
        if stage == 0:
            return [remote(
                buffer.at[0, core], buffer.at[0, core], send.at[0, 0], recv.at[0, 0], sibling
            )]
        axis = "xyz"[stage - 1]
        return [
            remote(
                buffer.at[stage, at[axis]], buffer.at[stage, at[axis]],
                send.at[stage, steps - 1], recv.at[stage, steps - 1], along(axis, steps),
            )
            for steps in (1, 2, 3)
        ]

    def sum_start(buffer, send, recv, stage, value):
        place = core if stage == 0 else at["xyz"[stage - 1]]
        buffer[stage, place] = value
        for copy in sum_copies(buffer, send, recv, stage):
            copy.start()

    def sum_finish(buffer, send, recv, stage):
        for copy in sum_copies(buffer, send, recv, stage):
            copy.wait()
        total = buffer[stage, 0] + buffer[stage, 1]
        if stage > 0:
            total = total + buffer[stage, 2] + buffer[stage, 3]
        return total

    sum_start(sm_v, sm_send, sm_recv, 0, small)

    def d_token_step(n, _):
        cols = columns_of(n)
        flat_v[:, cols] = c_v[:, cols].astype(F32) + dot(dqkv_v[...], w_v[cols, :], 1, 1)
        output_strips(flat_v, send_d, cols, low)
        return 0

    for copy in halo_o:
        copy.wait()
    each_column(lambda cols: output_block(flat_v, came_o, oblk_v, cols, low))
    store_out = pltpu.make_async_copy(oblk_v, out_h, store_sem.at[0])
    store_out.start()

    for part in range(3):
        scatter_sum(0, part)
    lax.fori_loop(0, 2, d_token_step, 0)
    sum_start(sm_v, sm_send, sm_recv, 1, sum_finish(sm_v, sm_send, sm_recv, 0))
    for part in range(3):
        scatter_sum(1, part)
    lax.fori_loop(2, 4, d_token_step, 0)
    sum_start(sm_v, sm_send, sm_recv, 2, sum_finish(sm_v, sm_send, sm_recv, 1))
    for part in range(3):
        scatter_sum(2, part)
    fin_copy = remote(fin_v.at[0], fin_v.at[1], fin_sem.at[0], fin_sem.at[1], sibling)
    fin_copy.start()
    squares = fin_v[0] * fin_v[0]
    squares = squares[:8] + squares[8:16] + squares[16:]
    squares = sum(squares[:, 128 * n : 128 * n + 128] for n in range(6))
    sum_start(sq_v, sq_send, sq_recv, 0, squares)
    lax.fori_loop(4, 6, d_token_step, 0)
    halo_d = halo(send_d, came_d, 3, 1)
    for copy in halo_d:
        copy.start()
    sum_start(sm_v, sm_send, sm_recv, 3, sum_finish(sm_v, sm_send, sm_recv, 2))
    for stage in (1, 2, 3):
        sum_start(sq_v, sq_send, sq_recv, stage, sum_finish(sq_v, sq_send, sq_recv, stage - 1))

    for copy in halo_d:
        copy.wait()
    each_column(lambda cols: output_block(flat_v, came_d, dblk_v, cols, low))
    store_dtok = pltpu.make_async_copy(dblk_v, dtok_h, store_sem.at[1])
    store_dtok.start()

    small = sum_finish(sm_v, sm_send, sm_recv, 3)
    squares = sum_finish(sq_v, sq_send, sq_recv, 3)
    total = jnp.sum(squares, axis=(0, 1), keepdims=True)
    total = total + jnp.sum(small * small, axis=(0, 1), keepdims=True)
    factor = jnp.minimum(1.0, jnp.sqrt(PARAMS / (total + clip_epsilon)))
    drel_ref[...] = small[:24] * factor
    for n in range(GROUPS):
        dgain_ref[:, LANES * n : LANES * n + LANES] = small[24 + n : 25 + n] * factor
        dshift_ref[:, LANES * n : LANES * n + LANES] = small[32 + n : 33 + n] * factor
    fin_copy.wait()
    own, other = fin_v[0] * factor, fin_v[1] * factor
    own = jnp.where(core == 0, own[:12], own[12:])
    other = jnp.where(core == 0, other[:12], other[12:])
    dpw_ref[:, :HALF] = jnp.where(core == 0, own, other)
    dpw_ref[:, HALF:] = jnp.where(core == 0, other, own)
    store_out.wait()
    store_dtok.wait()


def on_device(tokens, qkv_weight, rel_bias, proj_weight, norm_gain, norm_shift, cotangent):
    rel = jnp.pad(rel_bias, ((0, 0), (0, 1), (0, 1))).reshape(HEADS, 256)
    anywhere = pl.BlockSpec(memory_space=pl.ANY)
    vmem = pl.BlockSpec(memory_space=pltpu.VMEM)
    dma = pltpu.SemaphoreType.DMA
    strips = [pltpu.VMEM((112, D), BF)] * 8
    scratch = [
        pltpu.VMEM((16, 16, D), BF),
        pltpu.VMEM((16, 16, D), BF),
        pltpu.VMEM((D, 3 * D), BF),
        pltpu.VMEM((D, D), BF),
        pltpu.VMEM((TOKENS, D), BF),
        pltpu.VMEM((TOKENS, D), BF),
        pltpu.VMEM((18, TOKENS, LANES), BF),
        pltpu.VMEM((GROUPS, WINDOWS, CELLS, LANES), F32),
        pltpu.VMEM((TOKENS, D), BF),
        pltpu.VMEM((2, D, TOKENS), BF),
        pltpu.VMEM((TOKENS, D), F32),
        pltpu.VMEM((TOKENS, D), F32),
        pltpu.VMEM((TOKENS, D), BF),
        pltpu.VMEM((TOKENS, HALF), BF),
        pltpu.VMEM((GROUPS, TOKENS, LANES), BF),
        pltpu.VMEM((TOKENS, 3 * D), BF),
        pltpu.VMEM((16, 16, D), BF),
        pltpu.VMEM((16, 16, D), BF),
        pltpu.VMEM((1024, LANES), BF),
        pltpu.VMEM((HEADS, 8, 128), F32),
        pltpu.VMEM((GROUPS, CELLS, LANES), F32),
        pltpu.VMEM((CELLS, LANES), F32),
        pltpu.VMEM((HEADS, 8, 128), F32),
        pltpu.VMEM((2, 8, D), F32),
        *strips,
        pltpu.VMEM((3, 2, 4, 4, 2, 48, 128), BF),
        pltpu.VMEM((2, 3, 2, 4, 2, 48, 128), BF),
        pltpu.VMEM((3, 4, 4, 48, 128), BF),
        pltpu.VMEM((2, 4, 2, 48, 128), BF),
        pltpu.VMEM((2, 4, 2, 48, 128), BF),
        pltpu.VMEM((4, 4, 48, 128), BF),
        pltpu.VMEM((3, 2, 2, 48, 128), BF),
        pltpu.VMEM((3, 4, 48, 128), BF),
        pltpu.VMEM((3, 4, 48, 128), BF),
        pltpu.VMEM((2, 2, 48, 128), F32),
        pltpu.VMEM((4, 48, 128), F32),
        pltpu.VMEM((4, 48, 128), F32),
        pltpu.VMEM((3, 3, 48, 128), F32),
        pltpu.VMEM((2, 24, HALF), F32),
        pltpu.VMEM((4, 4, 40, LANES), F32),
        pltpu.VMEM((4, 4, 8, 128), F32),
        dma((3,)),
        dma((18,)),
        dma((2,)),
        dma((4, 3)),
        dma((4, 3)),
        dma((GROUPS,)),
        dma((GROUPS,)),
        dma((2,)),
        dma((3, 3, 3)),
        dma((3, 3, 3)),
        dma((4, 3)),
        dma((4, 3)),
        dma((4, 3)),
        dma((4, 3)),
        dma((2,)),
    ]
    out, d_tokens, d_proj, d_rel, d_gain, d_shift = pl.pallas_call(
        sublayer,
        out_shape=(
            jax.ShapeDtypeStruct((16, 16, D), BF),
            jax.ShapeDtypeStruct((16, 16, D), BF),
            jax.ShapeDtypeStruct((12, D), F32),
            jax.ShapeDtypeStruct((HEADS, LANES), F32),
            jax.ShapeDtypeStruct((1, D), F32),
            jax.ShapeDtypeStruct((1, D), F32),
        ),
        in_specs=[anywhere, anywhere, vmem, anywhere, vmem, vmem, anywhere],
        out_specs=(anywhere, anywhere, vmem, vmem, vmem, vmem),
        scratch_shapes=scratch,
        compiler_params=pltpu.CompilerParams(
            collective_id=0, has_side_effects=True, vmem_limit_bytes=60 * 2**20
        ),
        name="sublayer",
    )(
        tokens, qkv_weight, rel, proj_weight,
        norm_gain.reshape(1, D), norm_shift.reshape(1, D), cotangent,
    )
    d_rel = d_rel.reshape(HEADS, 16, 16)[:, :15, :15]
    return out, d_tokens, d_proj, d_rel, d_gain.reshape(D), d_shift.reshape(D)


def solution(mesh):
    in_specs = (P("lat", "lon", None), P(), P(), P(), P(), P(), P("lat", "lon", None))
    out_specs = (
        P("lat", "lon", None),
        P("lat", "lon", None),
        P(("lon", "lat"), None),
        P(),
        P(),
        P(),
    )
    return jax.shard_map(
        on_device, mesh=mesh, in_specs=in_specs, out_specs=out_specs, check_vma=False
    )
```

time: 772 us -> 99.9 us (0.13)
  blocking collectives: 441 us -> 0 us
  starting transfers between devices: 135 us -> 0 us
  local copies, waits for them, and re-layouts: 98.1 us -> 11.5 us
  Pallas kernels: 0 us -> 84.5 us
  matrix products: 57.8 us -> 0 us
  waiting for transfers between devices: 13.4 us -> 0 us
  other arithmetic: 15.1 us -> 2.62 us
    unnamed x1 -> x0, blocking collectives: 378 us -> none
    unnamed x32 -> x0, starting transfers between devices: 90.2 us -> none
    pallas_call x0 -> x1, Pallas kernels: none -> 84.5 us  [on_device(): pl.pallas_call(sublayer, out_shape=(jax.ShapeDtypeStruct((16, 16, D), BF)...]
    psum x1 -> x0, blocking collectives: 63.3 us -> none  [on_device(): spread_squares = lax.psum(shard_squares, ('lon', 'lat'))]
    dot_general x12 -> x0, matrix products: 52.3 us -> none  [the longest x1 9.65 us: on_device(): lax.dot_general(d_qkv, qkv_weight, (((1,), (1,)), ((), ())), preferred_el...]
    unnamed x99 -> x4, local copies, waits for them, and re-layouts: 57 us -> 6.48 us
    ppermute x8 -> x0, starting transfers between devices: 44.6 us -> none  [from_behind(): return lax.ppermute(value, axis, pairs)]
    reshape x14 -> x4, local copies, waits for them, and re-layouts: 22.4 us -> 4.11 us  [the longest x1 1.29 us: on_device(): norm_gain.reshape(1, D)]
  transfers between devices with their start and end apart: 40 -> 0, of which waited for: 3 -> 0; matrix products, arithmetic and copies ran while one was open for 15% -> 0% of each run, Pallas kernels for 0% -> 0%
where the time goes in v1:
time: 99.9 us; the launch traced here: 99.3 us
  Pallas kernels  84.5 us (85%)
  local copies, waits for them, and re-layouts  11.5 us (12%)
  other arithmetic  2.62 us (3%)
    pallas_call x1, Pallas kernels, on_device(): pl.pallas_call(sublayer, out_shape=(jax.ShapeDtypeStruct((16, 16, D), BF)...  84.5 us
    unnamed x4, local copies, waits for them, and re-layouts  6.48 us
    pallas_call x2, other arithmetic, on_device(): pl.pallas_call(sublayer, out_shape=(jax.ShapeDtypeStruct((16, 16, D), BF)...  2.62 us

profile of v1, /device:TPU:0, one launch (start us, length us, event | category | flops | bytes accessed | tf_op | source)
XLA Modules:
  0.0 99.3 jit_solution(10876368195413879145)
XLA Ops:
  0.6 0.9 pad.4
  1.6 0.7 copy.17.rel_ref
  2.2 1.3 %reshape.31.gain_ref = f32[1,1536]{1,0:T(1,128)} reshape(f32[1536]{0:T(1024)} %param.11) | data formatting | bytes 12288 | tf_op jit(solution)/shard_map/reshape | solution.py:688
  3.5 1.3 %reshape.32.shift_ref = f32[1,1536]{1,0:T(1,128)} reshape(f32[1536]{0:T(1024)} %param.12) | data formatting | bytes 12288 | tf_op jit(solution)/shard_map/reshape | solution.py:688
  4.8 84.5 %sublayer.1 = (bf16[16,16,1536]{2,1,0:T(8,128)(2,1)}, bf16[16,16,1536]{2,1,0:T(8,128)(2,1)}, f32[12,1536]{1,0:T(8,128)}, f32[24,256]{1,0:T(8,128)}, f32[1,1536]{1,0:T(1,128)}, /*index=5*/f32[1,1536]{1,0:T(1,128)}) custom-call(bf16[16,16,1536]{2,1,0:T(8,128)(2,1)} %tok_h.1, bf16[1536,4608]{1,0:T(8,128)(2,1)} %wq_h.1, f32[24,256]{1,0:T(8,128)} %copy.17.rel_ref, ...), custom_call_target="tpu_custom_call" | custom-call | tf_op jit(solution)/shard_map/sublayer/pallas_call | solution.py:669
  89.4 0.8 reshape.33
  90.2 0.8 copy.16
  91.0 1.3 %reduce = f32[1536]{0:T(1024)} reduce(f32[1,1536]{1,0:T(1,128)} %get-tuple-element.16, f32[]{:T(128)} %constant.7), dimensions={0}, to_apply=%get-tuple-element.16.reduce_sub_computation | reduce | bytes 12292 | tf_op jit(solution)/shard_map/sublayer/pallas_call | solution.py:669
  92.4 1.3 %reduce.1 = f32[1536]{0:T(1024)} reduce(f32[1,1536]{1,0:T(1,128)} %get-tuple-element.17, f32[]{:T(128)} %constant.7), dimensions={0}, to_apply=%get-tuple-element.17.reduce_sub_computation | reduce | bytes 12292 | tf_op jit(solution)/shard_map/sublayer/pallas_call | solution.py:669
  93.7 2.1 %copy.21 = bf16[16,16,1536]{2,1,0:T(8,128)(2,1)} copy(bf16[16,16,1536]{2,1,0:T(8,128)(2,1)} %get-tuple-element.30) | data formatting | bytes 1572864
  95.7 2.1 %copy.22 = bf16[16,16,1536]{2,1,0:T(8,128)(2,1)} copy(bf16[16,16,1536]{2,1,0:T(8,128)(2,1)} %get-tuple-element.31) | data formatting | bytes 1572864
  97.8 1.5 %copy.23 = f32[12,1536]{1,0:T(8,128)} copy(f32[12,1536]{1,0:T(8,128)} %get-tuple-element.32) | data formatting | bytes 147456

commit v2 on v1

--- a/solution.py
+++ b/solution.py
@@ -30,12 +30,12 @@
     return lax.dot_general(a, b, (((ca,), (cb,)), ((), ())), preferred_element_type=F32)
 
 
-def dot_exact(a, b, cb):
+def dot_exact(a, b, ca, cb):
     total = None
     for _ in range(3):
         part = a.astype(BF)
         a = a - part.astype(F32)
-        term = dot(part, b, 1, cb)
+        term = dot(part, b, ca, cb)
         total = term if total is None else total + term
     return total
 
@@ -180,12 +180,12 @@
     out_h, dtok_h, dpw_ref, drel_ref, dgain_ref, dshift_ref,
     tok_v, cot_v, w_v, pw_v, x_v, c_v, qkv_v, pt_v, mix_v, mixt_v, proj_v, flat_v,
     dp_v, dps_v, dmix_v, dqkv_v, oblk_v, dblk_v,
-    e_v, wb_v, bt_v, mask_v, u_v, acc_v,
+    e_v, rel_v, gain_v, shift_v, wb_v, bt_v, mask_v, u_v, acc_v,
     send_x, came_x, send_c, came_c, send_o, came_o, send_d, came_d,
     p_v, r1a, r1c, s2a, s2b, s2c, r2a, r2b, r2c, s3a, s3b, s3c, r3, fin_v,
-    sm_v, sq_v,
-    load_sem, w_sem, store_sem, halo_send, halo_recv, mix_send, mix_recv, dp_sem,
-    rs_send, rs_recv, sm_send, sm_recv, sq_send, sq_recv, fin_sem,
+    sm_v, sq1_v, sq2_v,
+    load_sem, w_sem, store_sem, halo_send, halo_recv, mix_send, mix_recv, dp_send, dp_recv,
+    rs_send, rs_recv, sm_send, sm_recv, sq_send, sq_recv, last_send, last_recv, last_store, fin_sem,
 ):
     lon = lax.axis_index("lon")
     lat = lax.axis_index("lat")
@@ -234,7 +234,15 @@
     load_cot.start()
 
     partners = [shifted(0, 1), shifted(0, -1), shifted(1, 0), shifted(-1, 0), shifted(1, 1), shifted(-1, -1)]
-    partners += [along(axis, steps) for axis in "xyz" for steps in (1, 2, 3)] + [sibling]
+    for k in range(1, 16):
+        chip = dict(at)
+        chip["x"] = lax.rem(at["x"] + k // 4, 4)
+        chip["y"] = lax.rem(at["y"] + k % 4, 4)
+        partners.append(device(chip, core))
+    for k in range(1, 8):
+        chip = dict(at)
+        chip["z"] = lax.rem(at["z"] + k // 2, 4)
+        partners.append(device(chip, core if k % 2 == 0 else 1 - core))
     barrier = pltpu.get_barrier_semaphore()
     for partner in partners:
         pl.semaphore_signal(barrier, inc=1, device_id=partner, device_id_type=MESH)
@@ -277,9 +285,12 @@
     for cj in range(8):
         hit = ((spot >> 3) == (slot >> 4)) & ((spot & 7) - cj + 7 == (slot & 15))
         e_v[128 * cj : 128 * cj + 128, :] = jnp.where(hit, 1.0, 0.0).astype(BF)
-    rel = rel_ref[...]
+    rel_v[...] = jnp.zeros_like(rel_v)
+    for a in range(15):
+        rel_v[16 * a : 16 * a + 15, :] = rel_ref[a]
+    rel = rel_v[...]
     for cj in range(8):
-        wb_v[:, cj, :] = dot_exact(rel, e_v[128 * cj : 128 * cj + 128, :], 1)
+        wb_v[:, cj, :] = dot_exact(rel, e_v[128 * cj : 128 * cj + 128, :], 0, 1)
     left8 = lax.broadcasted_iota(jnp.int32, (8, 128), 1) < 64
 
     def bias_step(g, _):
@@ -305,18 +316,6 @@
         copy.wait()
     each_column(lambda cols: input_windows(tok_v, came_x, x_v, cols, low))
 
-    def qkv_step(g, _):
-        for part in range(3):
-            chunk = part * GROUPS + g
-            load_w(chunk).wait()
-            value = dot(x_v[...], w_v[:, columns_of(chunk)], 1, 0).astype(BF)
-            if part == 0:
-                value = value * jnp.asarray(0.125, BF)
-            qkv_v[chunk] = value
-        return 0
-
-    lax.fori_loop(0, GROUPS, qkv_step, 0)
-
     lane_head = lax.broadcasted_iota(jnp.int32, (CELLS, LANES), 1) >> 6
     left = lax.broadcasted_iota(jnp.int32, (CELLS, 128), 1) < 64
 
@@ -326,24 +325,47 @@
             mixt_v.at[0, rows], mixt_v.at[1, rows], mix_send.at[g], mix_recv.at[g], sibling
         )
 
-    def forward_step(g, _):
+    def make_qkv(g):
+        for part in range(3):
+            chunk = part * GROUPS + g
+            value = dot(x_v[...], w_v[:, columns_of(chunk)], 1, 0).astype(BF)
+            if part == 0:
+                value = value * jnp.asarray(0.125, BF)
+            qkv_v[chunk] = value
+
+    def wait_weights(g):
+        for part in range(3):
+            load_w(part * GROUPS + g).wait()
+
+    def attend(g):
+        bias = bt_v[g]
+        masked = bias + mask_v[...]
+        mixed = []
         for w in range(WINDOWS):
             rows = slice(CELLS * w, CELLS * w + CELLS)
             q, k, v = [qkv_v[part * GROUPS + g, rows, :] for part in range(3)]
-            scores = dot(k, block_diagonal(q, lane_head), 1, 1) + bt_v[g]
-            if w >= 2:
-                scores = scores + mask_v[...]
+            scores = dot(k, block_diagonal(q, lane_head), 1, 1) + (bias if w < 2 else masked)
             peak = jnp.max(scores, axis=0, keepdims=True)
             raised = jnp.exp(scores - peak)
             shares = raised * (1.0 / jnp.sum(raised, axis=0, keepdims=True))
             pt_v[g, w] = shares
-            mixed = diagonal(dot(shares.astype(BF), v, 0, 0), left)
-            mix_v[rows, columns_of(g)] = mixed.astype(BF)
-        mixt_v[0, columns_of(g), :] = mix_v[:, columns_of(g)].T
+            mixed.append(diagonal(dot(shares.astype(BF), v, 0, 0), left).astype(BF))
+        mixed = stack(*mixed)
+        mix_v[:, columns_of(g)] = mixed
+        mixt_v[0, columns_of(g), :] = mixed.T
+
+    def forward_step(g, _):
+        wait_weights(g + 1)
+        attend(g)
+        make_qkv(g + 1)
         mix_copy(g).start()
         return 0
 
-    lax.fori_loop(0, GROUPS, forward_step, 0)
+    wait_weights(0)
+    make_qkv(0)
+    lax.fori_loop(0, GROUPS - 1, forward_step, 0)
+    attend(GROUPS - 1)
+    mix_copy(GROUPS - 1).start()
 
     def project_step(n, _):
         cols = columns_of(n)
@@ -358,42 +380,43 @@
     each_column(lambda cols: input_windows(cot_v, came_c, c_v, cols, low))
 
     acc_v[...] = jnp.zeros_like(acc_v)
+    gain = gain_ref[...].reshape(1, D)
+    shift = shift_ref[...].reshape(1, D)
+    gain_v[...] = gain
+    shift_v[...] = shift
+
+    other_half = pl.ds(pl.multiple_of((1 - core) * HALF, HALF), HALF)
+
+    def dp_copy(m):
+        rows = pl.ds(pl.multiple_of(m * CELLS, CELLS), CELLS)
+        return remote(dp_v.at[rows, other_half], dps_v.at[rows], dp_send.at[m], dp_recv.at[m], sibling)
 
     def norm_step(m, _):
-        rows = pl.ds(pl.multiple_of(m * 16, 16), 16)
-        projected = proj_v[rows, :]
-        centre = projected - jnp.mean(projected, axis=1, keepdims=True)
-        inverse = lax.rsqrt(jnp.mean(centre * centre, axis=1, keepdims=True) + norm_epsilon)
-        normed = centre * inverse
-        flat_v[rows, :] = x_v[rows, :].astype(F32) + normed * gain_ref[...] + shift_ref[...]
-        upstream = c_v[rows, :].astype(F32)
-        product = upstream * normed
-        acc_v[0] += product[:8] + product[8:]
-        acc_v[1] += upstream[:8] + upstream[8:]
-        d_normed = upstream * gain_ref[...]
-        inner = d_normed - jnp.mean(d_normed, axis=1, keepdims=True)
-        inner = inner - normed * jnp.mean(d_normed * normed, axis=1, keepdims=True)
-        dp_v[rows, :] = (inverse * inner).astype(BF)
+        sums = [None, None]
+        for part in range(4):
+            rows = pl.ds(pl.multiple_of(m * CELLS + 16 * part, 16), 16)
+            projected = proj_v[rows, :]
+            centre = projected - jnp.mean(projected, axis=1, keepdims=True)
+            inverse = lax.rsqrt(jnp.mean(centre * centre, axis=1, keepdims=True) + norm_epsilon)
+            normed = centre * inverse
+            flat_v[rows, :] = x_v[rows, :].astype(F32) + normed * gain_v[...] + shift_v[...]
+            upstream = c_v[rows, :].astype(F32)
+            product = upstream * normed
+            terms = (product[:8] + product[8:], upstream[:8] + upstream[8:])
+            sums = [b if a is None else a + b for a, b in zip(sums, terms)]
+            d_normed = upstream * gain_v[...]
+            inner = d_normed - jnp.mean(d_normed, axis=1, keepdims=True)
+            inner = inner - normed * jnp.mean(d_normed * normed, axis=1, keepdims=True)
+            dp_v[rows, :] = (inverse * inner).astype(BF)
+        acc_v[0] += sums[0]
+        acc_v[1] += sums[1]
+        dp_copy(m).start()
         return 0
 
-    lax.fori_loop(0, TOKENS // 16, norm_step, 0)
-
-    other_half = pl.ds(pl.multiple_of((1 - core) * HALF, HALF), HALF)
-    dp_copy = remote(dp_v.at[:, other_half], dps_v, dp_sem.at[0], dp_sem.at[1], sibling)
-    dp_copy.start()
-
-    each_column(lambda cols: output_strips(flat_v, send_o, cols, low))
-    halo_o = halo(send_o, came_o, 2, 1)
-    for copy in halo_o:
-        copy.start()
-
-    def d_mixed_step(n, _):
-        dmix_v[n] = dot(dp_v[...], pw_v[columns_of(n), :], 1, 1).astype(BF)
-        return 0
-
-    lax.fori_loop(0, GROUPS, d_mixed_step, 0)
-
-    dp_copy.wait()
+    lax.fori_loop(0, TOKENS // CELLS, norm_step, 0)
+
+    for m in range(WINDOWS):
+        dp_copy(m).wait()
     for g in range(GROUPS):
         mix_copy(g).wait()
 
@@ -465,6 +488,17 @@
                 2, 4, 2, 48, 128
             )
         scatter_start(0, part)
+
+    each_column(lambda cols: output_strips(flat_v, send_o, cols, low))
+    halo_o = halo(send_o, came_o, 2, 1)
+    for copy in halo_o:
+        copy.start()
+
+    def d_mixed_step(n, _):
+        dmix_v[n] = dot(dp_v[...], pw_v[columns_of(n), :], 1, 1).astype(BF)
+        return 0
+
+    lax.fori_loop(0, GROUPS, d_mixed_step, 0)
 
     def backward_step(g, _):
         total = None
@@ -500,7 +534,7 @@
 
     small = None
     for cj in range(8):
-        term = dot_exact(u_v[:, cj, :], e_v[128 * cj : 128 * cj + 128, :], 0)
+        term = dot_exact(u_v[:, cj, :], e_v[128 * cj : 128 * cj + 128, :], 1, 0)
         small = term if small is None else small + term
     gain_sum = jnp.sum(acc_v[0], axis=0, keepdims=True)
     shift_sum = jnp.sum(acc_v[1], axis=0, keepdims=True)
@@ -541,10 +575,74 @@
 
     sum_start(sm_v, sm_send, sm_recv, 0, small)
 
+    def squares_copies(stage):
+        copies = []
+        if stage == 1:
+            mine = sq1_v.at[at["x"] * 4 + at["y"]]
+            for k in range(1, 16):
+                chip = dict(at)
+                chip["x"] = lax.rem(at["x"] + k // 4, 4)
+                chip["y"] = lax.rem(at["y"] + k % 4, 4)
+                copies.append(
+                    remote(mine, mine, sq_send.at[0, k - 1], sq_recv.at[0, k - 1], device(chip, core))
+                )
+        else:
+            mine = sq2_v.at[at["z"] * 2 + core]
+            for k in range(1, 8):
+                chip = dict(at)
+                chip["z"] = lax.rem(at["z"] + k // 2, 4)
+                on_core = core if k % 2 == 0 else 1 - core
+                copies.append(
+                    remote(mine, mine, sq_send.at[1, k - 1], sq_recv.at[1, k - 1], device(chip, on_core))
+                )
+        return copies
+
+    def squares_start(stage, value):
+        if stage == 1:
+            sq1_v[at["x"] * 4 + at["y"]] = value
+        else:
+            sq2_v[at["z"] * 2 + core] = value
+        for copy in squares_copies(stage):
+            copy.start()
+
+    def squares_finish(stage):
+        for copy in squares_copies(stage):
+            copy.wait()
+        buffer, count = (sq1_v, 16) if stage == 1 else (sq2_v, 8)
+        total = buffer[0]
+        for k in range(1, count):
+            total = total + buffer[k]
+        return total
+
+    def halo_d(n):
+        cols = columns_of(n)
+        rows = (slice(0, 48), slice(48, 96), slice(96, 112))
+        targets = (shifted(0, 1), shifted(1, 0), shifted(1, 1))
+        return [
+            remote(
+                send_d.at[rows[i], cols], came_d.at[rows[i], cols],
+                last_send.at[n, i], last_recv.at[n, i], targets[i],
+            )
+            for i in range(3)
+        ]
+
+    def store_d(n):
+        cols = columns_of(n)
+        return pltpu.make_async_copy(dblk_v.at[:, :, cols], dtok_h.at[:, :, cols], last_store.at[n])
+
+    def last_step(n, _):
+        for copy in halo_d(n):
+            copy.wait()
+        output_block(flat_v, came_d, dblk_v, columns_of(n), low)
+        store_d(n).start()
+        return 0
+
     def d_token_step(n, _):
         cols = columns_of(n)
         flat_v[:, cols] = c_v[:, cols].astype(F32) + dot(dqkv_v[...], w_v[cols, :], 1, 1)
         output_strips(flat_v, send_d, cols, low)
+        for copy in halo_d(n):
+            copy.start()
         return 0
 
     for copy in halo_o:
@@ -568,30 +666,24 @@
     squares = fin_v[0] * fin_v[0]
     squares = squares[:8] + squares[8:16] + squares[16:]
     squares = sum(squares[:, 128 * n : 128 * n + 128] for n in range(6))
-    sum_start(sq_v, sq_send, sq_recv, 0, squares)
+    squares_start(1, squares)
     lax.fori_loop(4, 6, d_token_step, 0)
-    halo_d = halo(send_d, came_d, 3, 1)
-    for copy in halo_d:
-        copy.start()
     sum_start(sm_v, sm_send, sm_recv, 3, sum_finish(sm_v, sm_send, sm_recv, 2))
-    for stage in (1, 2, 3):
-        sum_start(sq_v, sq_send, sq_recv, stage, sum_finish(sq_v, sq_send, sq_recv, stage - 1))
-
-    for copy in halo_d:
-        copy.wait()
-    each_column(lambda cols: output_block(flat_v, came_d, dblk_v, cols, low))
-    store_dtok = pltpu.make_async_copy(dblk_v, dtok_h, store_sem.at[1])
-    store_dtok.start()
+    squares = squares_finish(1)
+    squares_start(2, squares)
+    lax.fori_loop(0, GROUPS, last_step, 0)
 
     small = sum_finish(sm_v, sm_send, sm_recv, 3)
-    squares = sum_finish(sq_v, sq_send, sq_recv, 3)
+    squares = squares_finish(2)
     total = jnp.sum(squares, axis=(0, 1), keepdims=True)
     total = total + jnp.sum(small * small, axis=(0, 1), keepdims=True)
     factor = jnp.minimum(1.0, jnp.sqrt(PARAMS / (total + clip_epsilon)))
-    drel_ref[...] = small[:24] * factor
+    drel = (small[:24] * factor).T
+    for a in range(15):
+        drel_ref[a] = drel[16 * a : 16 * a + 15]
     for n in range(GROUPS):
-        dgain_ref[:, LANES * n : LANES * n + LANES] = small[24 + n : 25 + n] * factor
-        dshift_ref[:, LANES * n : LANES * n + LANES] = small[32 + n : 33 + n] * factor
+        dgain_ref[LANES * n : LANES * n + LANES] = (small[24 + n : 25 + n] * factor).reshape(LANES)
+        dshift_ref[LANES * n : LANES * n + LANES] = (small[32 + n : 33 + n] * factor).reshape(LANES)
     fin_copy.wait()
     own, other = fin_v[0] * factor, fin_v[1] * factor
     own = jnp.where(core == 0, own[:12], own[12:])
@@ -599,11 +691,20 @@
     dpw_ref[:, :HALF] = jnp.where(core == 0, own, other)
     dpw_ref[:, HALF:] = jnp.where(core == 0, other, own)
     store_out.wait()
-    store_dtok.wait()
+    for n in range(GROUPS):
+        store_d(n).wait()
+
+
+def hand_over(*refs):
+    sems = refs[12]
+    copies = [pltpu.make_async_copy(refs[i], refs[6 + i], sems.at[i]) for i in range(6)]
+    for copy in copies:
+        copy.start()
+    for copy in copies:
+        copy.wait()
 
 
 def on_device(tokens, qkv_weight, rel_bias, proj_weight, norm_gain, norm_shift, cotangent):
-    rel = jnp.pad(rel_bias, ((0, 0), (0, 1), (0, 1))).reshape(HEADS, 256)
     anywhere = pl.BlockSpec(memory_space=pl.ANY)
     vmem = pl.BlockSpec(memory_space=pltpu.VMEM)
     dma = pltpu.SemaphoreType.DMA
@@ -628,6 +729,9 @@
         pltpu.VMEM((16, 16, D), BF),
         pltpu.VMEM((16, 16, D), BF),
         pltpu.VMEM((1024, LANES), BF),
+        pltpu.VMEM((LANES, HEADS), F32),
+        pltpu.VMEM((1, D), F32),
+        pltpu.VMEM((1, D), F32),
         pltpu.VMEM((HEADS, 8, 128), F32),
         pltpu.VMEM((GROUPS, CELLS, LANES), F32),
         pltpu.VMEM((CELLS, LANES), F32),
@@ -649,32 +753,37 @@
         pltpu.VMEM((3, 3, 48, 128), F32),
         pltpu.VMEM((2, 24, HALF), F32),
         pltpu.VMEM((4, 4, 40, LANES), F32),
-        pltpu.VMEM((4, 4, 8, 128), F32),
+        pltpu.VMEM((16, 8, 128), F32),
+        pltpu.VMEM((8, 8, 128), F32),
         dma((3,)),
         dma((18,)),
-        dma((2,)),
-        dma((4, 3)),
-        dma((4, 3)),
+        dma((1,)),
+        dma((3, 3)),
+        dma((3, 3)),
         dma((GROUPS,)),
         dma((GROUPS,)),
-        dma((2,)),
+        dma((WINDOWS,)),
+        dma((WINDOWS,)),
         dma((3, 3, 3)),
         dma((3, 3, 3)),
         dma((4, 3)),
         dma((4, 3)),
-        dma((4, 3)),
-        dma((4, 3)),
+        dma((2, 15)),
+        dma((2, 15)),
+        dma((GROUPS, 3)),
+        dma((GROUPS, 3)),
+        dma((GROUPS,)),
         dma((2,)),
     ]
-    out, d_tokens, d_proj, d_rel, d_gain, d_shift = pl.pallas_call(
+    results = pl.pallas_call(
         sublayer,
         out_shape=(
             jax.ShapeDtypeStruct((16, 16, D), BF),
             jax.ShapeDtypeStruct((16, 16, D), BF),
             jax.ShapeDtypeStruct((12, D), F32),
-            jax.ShapeDtypeStruct((HEADS, LANES), F32),
-            jax.ShapeDtypeStruct((1, D), F32),
-            jax.ShapeDtypeStruct((1, D), F32),
+            jax.ShapeDtypeStruct((15, 15, HEADS), F32),
+            jax.ShapeDtypeStruct((D,), F32),
+            jax.ShapeDtypeStruct((D,), F32),
         ),
         in_specs=[anywhere, anywhere, vmem, anywhere, vmem, vmem, anywhere],
         out_specs=(anywhere, anywhere, vmem, vmem, vmem, vmem),
@@ -684,11 +793,18 @@
         ),
         name="sublayer",
     )(
-        tokens, qkv_weight, rel, proj_weight,
-        norm_gain.reshape(1, D), norm_shift.reshape(1, D), cotangent,
+        tokens, qkv_weight, rel_bias.transpose(1, 2, 0), proj_weight, norm_gain, norm_shift, cotangent,
     )
-    d_rel = d_rel.reshape(HEADS, 16, 16)[:, :15, :15]
-    return out, d_tokens, d_proj, d_rel, d_gain.reshape(D), d_shift.reshape(D)
+    out, d_tokens, d_proj, d_rel, d_gain, d_shift = pl.pallas_call(
+        hand_over,
+        out_shape=tuple(jax.ShapeDtypeStruct(r.shape, r.dtype) for r in results),
+        in_specs=[anywhere] * 6,
+        out_specs=(anywhere,) * 6,
+        scratch_shapes=[dma((6,))],
+        compiler_params=pltpu.CompilerParams(vmem_limit_bytes=60 * 2**20),
+        name="hand_over",
+    )(*results)
+    return out, d_tokens, d_proj, d_rel.transpose(2, 0, 1), d_gain, d_shift
 
 
 def solution(mesh):

time: 99.9 us -> 131 us (1.31)
  Pallas kernels: 84.5 us -> 129 us
  local copies, waits for them, and re-layouts: 11.5 us -> 0 us
  other arithmetic: 2.62 us -> 0 us
    pallas_call x0 -> x1, Pallas kernels: none -> 55.6 us  [on_device(): pl.pallas_call(hand_over, out_shape=tuple((jax.ShapeDtypeStruct(r.shape,...]
    pallas_call x1, Pallas kernels: 84.5 us -> 73.3 us  [on_device(): pl.pallas_call(sublayer, out_shape=(jax.ShapeDtypeStruct((16, 16, D), BF)...]
    unnamed x4 -> x0, local copies, waits for them, and re-layouts: 6.48 us -> none
    reshape x4 -> x0, local copies, waits for them, and re-layouts: 4.11 us -> none  [the longest x1 1.29 us: on_device(): norm_gain.reshape(1, D)]
    pallas_call x2 -> x0, other arithmetic: 2.62 us -> none  [on_device(): pl.pallas_call(sublayer, out_shape=(jax.ShapeDtypeStruct((16, 16, D), BF)...]
where the time goes in v2:
time: 131 us; the launch traced here: 130 us
  Pallas kernels  129 us (98%)
    pallas_call x1, Pallas kernels, on_device(): pl.pallas_call(sublayer, out_shape=(jax.ShapeDtypeStruct((16, 16, D), BF)...  73.3 us
    pallas_call x1, Pallas kernels, on_device(): pl.pallas_call(hand_over, out_shape=tuple((jax.ShapeDtypeStruct(r.shape,...  55.6 us

profile of v2, /device:TPU:0, one launch (start us, length us, event | category | flops | bytes accessed | tf_op | source)
XLA Modules:
  0.0 129.6 jit_solution(9298072626969073443)
XLA Ops:
  0.6 73.3 %sublayer.1 = (bf16[16,16,1536]{2,1,0:T(8,128)(2,1)}, bf16[16,16,1536]{2,1,0:T(8,128)(2,1)}, f32[12,1536]{1,0:T(8,128)}, f32[15,15,24]{2,1,0:T(8,128)}, f32[1536]{0:T(1024)}, /*index=5*/f32[1536]{0:T(1024)}) custom-call(bf16[16,16,1536]{2,1,0:T(8,128)(2,1)} %tok_h.1, bf16[1536,4608]{1,0:T(8,128)(2,1)} %wq_h.1, f32[15,15,24]{2,1,0:T(8,128)} %bitcast.2, ...), custom_call_target="tpu_custom_call" | custom-call | tf_op jit(solution)/shard_map/sublayer/pallas_call | solution.py:778
  74.0 55.6 %hand_over.1 = (bf16[16,16,1536]{2,1,0:T(8,128)(2,1)}, bf16[16,16,1536]{2,1,0:T(8,128)(2,1)}, f32[12,1536]{1,0:T(8,128)}, f32[15,15,24]{2,1,0:T(8,128)}, f32[1536]{0:T(1024)}, /*index=5*/f32[1536]{0:T(1024)}) custom-call(bf16[16,16,1536]{2,1,0:T(8,128)(2,1)} %get-tuple-element.18.refs_0_, bf16[16,16,1536]{2,1,0:T(8,128)(2,1)} %get-tuple-element.19.refs_1_, ...), custom_call_target="tpu_custom_call" | custom-call | tf_op jit(solution)/shard_map/hand_over/pallas_call | solution.py:798

commit v3 on v2

--- a/solution.py
+++ b/solution.py
@@ -66,92 +66,110 @@
     return pl.ds(pl.multiple_of(step * width, width), width)
 
 
+def pack_first(a, b):
+    return jnp.where(low_rows(a.shape[1]), a, turn(b))
+
+
+def pack_last(a, b):
+    return jnp.where(low_rows(a.shape[1]), turn(a), b)
+
+
+def four_pairs(pack, values):
+    return stack(pack(values[0], values[1]), pack(values[2], values[3])).astype(BF)
+
+
+STRIPS = (slice(0, 32), slice(32, 48), slice(48, 96), slice(96, 112))
+STRIP_STEPS = ((0, 1), (0, -1), (1, 0), (1, -1))
+
+
 def input_strips(block, strips, cols, low):
-    for k in range(3):
-        a, b, c, d = [row_halves(block, 4 + 4 * k + i, cols)[0] for i in range(4)]
-        strips[16 * k : 16 * k + 16, cols] = stack(
-            jnp.where(low, a, turn(b)), jnp.where(low, c, turn(d))
-        ).astype(BF)
+    for k in range(2):
+        rows = [row_halves(block, 4 + 4 * k + i, cols)[0] for i in range(4)]
+        strips[16 * k : 16 * k + 16, cols] = four_pairs(pack_first, rows)
+    rows = [row_halves(block, 12 + i, cols)[1] for i in range(4)]
+    strips[32:48, cols] = four_pairs(pack_last, rows)
     t = [row_halves(block, r, cols) for r in range(4)]
     wide = [turn(jnp.where(low, t1, t0)) for t0, t1 in t]
     strips[48:64, cols] = stack(wide[0], wide[1]).astype(BF)
     strips[64:80, cols] = stack(wide[2], wide[3]).astype(BF)
-    strips[80:96, cols] = stack(
-        jnp.where(low, turn(t[0][1]), t[1][1]), jnp.where(low, turn(t[2][1]), t[3][1])
-    ).astype(BF)
-    strips[96:112, cols] = stack(
-        jnp.where(low, t[0][0], turn(t[1][0])), jnp.where(low, t[2][0], turn(t[3][0]))
-    ).astype(BF)
+    strips[80:96, cols] = four_pairs(pack_first, [t0 for t0, _ in t])
+    strips[96:112, cols] = four_pairs(pack_last, [t1 for _, t1 in t])
+
+
+def own_windows(block, flat, cols, low):
+    for r, at in ((4, 0), (6, 16), (8, 32), (10, 48), (12, 192), (14, 208)):
+        t0, t1 = row_halves(block, r, cols)
+        u0, u1 = row_halves(block, r + 1, cols)
+        flat[at : at + 16, cols] = stack(
+            turn(jnp.where(low, t1, t0)), turn(jnp.where(low, u1, u0))
+        ).astype(BF)
 
 
 def input_windows(block, came, flat, cols, low):
-    for k in range(3):
+    for k in range(2):
         pairs = halves(came, slice(16 * k, 16 * k + 16), cols)
         for i in range(2):
             r = 4 * k + 2 * i
             s = pairs[i]
-            at = (r // 8) * 128 + (r % 8) * 8
-            t0, t1 = row_halves(block, r + 4, cols)
-            u0, u1 = row_halves(block, r + 5, cols)
-            flat[at : at + 16, cols] = stack(
-                turn(jnp.where(low, t1, t0)), turn(jnp.where(low, u1, u0))
-            ).astype(BF)
-            flat[at + 64 : at + 80, cols] = stack(
+            t1 = row_halves(block, r + 4, cols)[1]
+            u1 = row_halves(block, r + 5, cols)[1]
+            flat[64 + 8 * r : 80 + 8 * r, cols] = stack(
                 jnp.where(low, turn(t1), turn(s)), jnp.where(low, turn(u1), s)
             ).astype(BF)
+    west = halves(came, slice(32, 48), cols)
     side = halves(came, slice(80, 96), cols)
     corner = halves(came, slice(96, 112), cols)
     for i in range(2):
-        at = 128 + 32 + 16 * i
-        flat[at : at + 16, cols] = came[48 + 16 * i : 64 + 16 * i, cols]
+        t0 = row_halves(block, 12 + 2 * i, cols)[0]
+        u0 = row_halves(block, 13 + 2 * i, cols)[0]
+        s = west[i]
+        flat[128 + 16 * i : 144 + 16 * i, cols] = stack(
+            jnp.where(low, s, turn(t0)), jnp.where(low, turn(s), turn(u0))
+        ).astype(BF)
         s, d = side[i], corner[i]
-        flat[at + 64 : at + 80, cols] = stack(
-            jnp.where(low, s, turn(d)), jnp.where(low, turn(s), d)
+        flat[160 + 16 * i : 176 + 16 * i, cols] = stack(
+            jnp.where(low, d, turn(s)), jnp.where(low, turn(d), s)
         ).astype(BF)
-
-
-def output_strips(flat, strips, cols, low):
-    for k in range(3):
-        parts = []
-        for i in range(4):
-            r = 4 * k + i
-            at = (r // 8) * 128 + 64 + (r % 8) * 8
-            parts.append(flat[at : at + 8, cols])
-        a, b, c, d = parts
-        strips[16 * k : 16 * k + 16, cols] = stack(
-            jnp.where(low, turn(a), b), jnp.where(low, turn(c), d)
-        ).astype(BF)
-    strips[48:80, cols] = flat[160:192, cols].astype(BF)
-    a, b, c, d = [flat[224 + 8 * i : 232 + 8 * i, cols] for i in range(4)]
-    strips[80:96, cols] = stack(
-        jnp.where(low, a, turn(b)), jnp.where(low, c, turn(d))
-    ).astype(BF)
-    strips[96:112, cols] = stack(
-        jnp.where(low, turn(a), b), jnp.where(low, turn(c), d)
-    ).astype(BF)
+        flat[224 + 16 * i : 240 + 16 * i, cols] = came[48 + 16 * i : 64 + 16 * i, cols]
+
+
+def output_strips(flat, strips, cols):
+    def rows_of(start):
+        return [flat[start + 8 * i : start + 8 * i + 8, cols] for i in range(4)]
+
+    for k in range(2):
+        strips[16 * k : 16 * k + 16, cols] = four_pairs(pack_last, rows_of(64 + 32 * k))
+    strips[32:48, cols] = four_pairs(pack_first, rows_of(128))
+    strips[48:80, cols] = flat[224:256, cols].astype(BF)
+    strips[80:96, cols] = four_pairs(pack_last, rows_of(160))
+    strips[96:112, cols] = four_pairs(pack_first, rows_of(160))
 
 
 def output_block(flat, came, block, cols, low):
-    for k in range(3):
+    for k in range(2):
         pairs = halves(came, slice(16 * k, 16 * k + 16), cols)
         for i in range(4):
             r = 4 * k + i
             s = pairs[i // 2]
             s = s if i % 2 == 0 else turn(s)
-            at = (r // 8) * 128 + (r % 8) * 8
-            a = turn(flat[at : at + 8, cols])
-            b = turn(flat[at + 64 : at + 72, cols])
+            a = turn(flat[8 * r : 8 * r + 8, cols])
+            b = turn(flat[64 + 8 * r : 72 + 8 * r, cols])
             block[r + 4, :, cols] = stack(jnp.where(low, s, a), jnp.where(low, a, b)).astype(BF)
+    east = halves(came, slice(32, 48), cols)
     side = halves(came, slice(80, 96), cols)
     corner = halves(came, slice(96, 112), cols)
     for i in range(2):
         wides = halves(came, slice(48 + 16 * i, 64 + 16 * i), cols)
-        s, d = side[i], corner[i]
         for k in range(2):
+            r = 2 * i + k
+            a = turn(flat[128 + 8 * r : 136 + 8 * r, cols])
+            b = turn(flat[192 + 8 * r : 200 + 8 * r, cols])
+            s = turn(east[i]) if k == 0 else east[i]
+            block[12 + r, :, cols] = stack(jnp.where(low, a, b), jnp.where(low, b, s)).astype(BF)
             wide = turn(wides[k])
-            at_low = d if k == 0 else turn(d)
-            at_high = turn(s) if k == 0 else s
-            block[2 * i + k, :, cols] = stack(
+            at_low = side[i] if k == 0 else turn(side[i])
+            at_high = turn(corner[i]) if k == 0 else corner[i]
+            block[r, :, cols] = stack(
                 jnp.where(low, at_low, wide), jnp.where(low, wide, at_high)
             ).astype(BF)
 
@@ -183,9 +201,9 @@
     e_v, rel_v, gain_v, shift_v, wb_v, bt_v, mask_v, u_v, acc_v,
     send_x, came_x, send_c, came_c, send_o, came_o, send_d, came_d,
     p_v, r1a, r1c, s2a, s2b, s2c, r2a, r2b, r2c, s3a, s3b, s3c, r3, fin_v,
-    sm_v, sq1_v, sq2_v,
+    sm_v, sq_v,
     load_sem, w_sem, store_sem, halo_send, halo_recv, mix_send, mix_recv, dp_send, dp_recv,
-    rs_send, rs_recv, sm_send, sm_recv, sq_send, sq_recv, last_send, last_recv, last_store, fin_sem,
+    rs_send, rs_recv, sm_send, sm_recv, sq_send, sq_recv, last_store, fin_sem,
 ):
     lon = lax.axis_index("lon")
     lat = lax.axis_index("lat")
@@ -203,10 +221,10 @@
             "lat": lax.rem(z, 2) * 2 + on_core,
         }
 
-    def along(axis, steps):
+    def along(axis, steps, on_core=core):
         chip = dict(at)
         chip[axis] = lax.rem(at[axis] + steps, 4)
-        return device(chip, core)
+        return device(chip, on_core)
 
     sibling = device(at, 1 - core)
 
@@ -233,16 +251,12 @@
     load_tok.start()
     load_cot.start()
 
-    partners = [shifted(0, 1), shifted(0, -1), shifted(1, 0), shifted(-1, 0), shifted(1, 1), shifted(-1, -1)]
-    for k in range(1, 16):
-        chip = dict(at)
-        chip["x"] = lax.rem(at["x"] + k // 4, 4)
-        chip["y"] = lax.rem(at["y"] + k % 4, 4)
-        partners.append(device(chip, core))
-    for k in range(1, 8):
-        chip = dict(at)
-        chip["z"] = lax.rem(at["z"] + k // 2, 4)
-        partners.append(device(chip, core if k % 2 == 0 else 1 - core))
+    partners = [shifted(0, 1), shifted(0, -1), shifted(1, 0), shifted(-1, 0), shifted(1, -1), shifted(-1, 1)]
+    circles = [[along(axis, steps) for steps in (1, 2, 3)] for axis in "xy"]
+    circles.append(
+        [sibling] + [along("z", steps) for steps in (1, 2, 3)] + [along("z", steps, 1 - core) for steps in (1, 2, 3)]
+    )
+    partners += circles[0] + circles[1] + circles[2]
     barrier = pltpu.get_barrier_semaphore()
     for partner in partners:
         pl.semaphore_signal(barrier, inc=1, device_id=partner, device_id_type=MESH)
@@ -257,15 +271,14 @@
     def each_column(body):
         lax.fori_loop(0, GROUPS, lambda n, _: (body(columns_of(n)), 0)[1], 0)
 
-    def halo(strips, came, which, sign):
-        rows = (slice(0, 48), slice(48, 96), slice(96, 112))
-        targets = (shifted(0, sign), shifted(sign, 0), shifted(sign, sign))
+    def halo(strips, came, which, sign, cols=slice(None)):
         return [
             remote(
-                strips.at[rows[i]], came.at[rows[i]],
-                halo_send.at[which, i], halo_recv.at[which, i], targets[i],
+                strips.at[rows, cols], came.at[rows, cols],
+                halo_send.at[which, i], halo_recv.at[which, i],
+                shifted(sign * STRIP_STEPS[i][0], sign * STRIP_STEPS[i][1]),
             )
-            for i in range(3)
+            for i, rows in enumerate(STRIPS)
         ]
 
     load_tok.wait()
@@ -274,11 +287,13 @@
     halo_x = halo(send_x, came_x, 0, -1)
     for copy in halo_x:
         copy.start()
+    each_column(lambda cols: own_windows(tok_v, x_v, cols, low))
     load_cot.wait()
     each_column(lambda cols: input_strips(cot_v, send_c, cols, low))
     halo_c = halo(send_c, came_c, 1, -1)
     for copy in halo_c:
         copy.start()
+    each_column(lambda cols: own_windows(cot_v, c_v, cols, low))
 
     spot = lax.broadcasted_iota(jnp.int32, (128, LANES), 0)
     slot = lax.broadcasted_iota(jnp.int32, (128, LANES), 1)
@@ -415,6 +430,11 @@
 
     lax.fori_loop(0, TOKENS // CELLS, norm_step, 0)
 
+    each_column(lambda cols: output_strips(flat_v, send_o, cols))
+    halo_o = halo(send_o, came_o, 2, 1)
+    for copy in halo_o:
+        copy.start()
+
     for m in range(WINDOWS):
         dp_copy(m).wait()
     for g in range(GROUPS):
@@ -438,42 +458,54 @@
         (r3.at[0], r3.at[1], r3.at[2]),
     )
 
-    def scatter_copies(stage, part):
+    pieces = (slice(0, 32), slice(32, 48))
+
+    def scatter_copies(stage, part, piece):
         buffer, lead, axes = stages[stage][part]
         axis = ORDERS[part][stage]
+        rows = pieces[piece]
+        whole = (slice(None),) * (len(axes) - (2 if axis == "z" else 1))
         copies = []
         for steps in (1, 2, 3):
             index = lax.rem(at[axis] + steps, 4)
             copies.append(
                 remote(
-                    slot_of(buffer, lead, axes, axis, index),
-                    arrivals[stage][part].at[steps - 1],
-                    rs_send.at[stage, part, steps - 1],
-                    rs_recv.at[stage, part, steps - 1],
+                    slot_of(buffer, lead, axes, axis, index).at[whole + (rows,)],
+                    arrivals[stage][part].at[(steps - 1,) + whole + (rows,)],
+                    rs_send.at[stage, part, 3 * piece + steps - 1],
+                    rs_recv.at[stage, part, 3 * piece + steps - 1],
                     along(axis, steps),
                 )
             )
         return copies
 
-    def scatter_start(stage, part):
-        for copy in scatter_copies(stage, part):
+    def scatter_start(stage, part, piece):
+        for copy in scatter_copies(stage, part, piece):
             copy.start()
 
-    def scatter_sum(stage, part):
-        for copy in scatter_copies(stage, part):
+    def scatter_sum(stage, part, piece):
+        for copy in scatter_copies(stage, part, piece):
             copy.wait()
         buffer, lead, axes = stages[stage][part]
         axis = ORDERS[part][stage]
-        total = slot_of(buffer, lead, axes, axis, at[axis])[...].astype(F32)
+        rows = pieces[piece]
+        whole = (slice(None),) * (len(axes) - (2 if axis == "z" else 1))
+        total = slot_of(buffer, lead, axes, axis, at[axis])[whole + (rows,)].astype(F32)
         for steps in range(3):
-            total = total + arrivals[stage][part][steps].astype(F32)
+            total = total + arrivals[stage][part][(steps,) + whole + (rows,)].astype(F32)
         if stage < 2:
             target = stages[stage + 1][part][0]
-            target[...] = total.astype(target.dtype)
-            scatter_start(stage + 1, part)
+            target[whole + (rows,)] = total.astype(target.dtype)
+            scatter_start(stage + 1, part, piece)
+        elif piece == 0:
+            fin_v[0, :, LANES * part : LANES * part + 128] = total[:24]
+            fin_v[0, :8, LANES * part + 128 : LANES * part + 256] = total[24:]
         else:
-            fin_v[0, :, LANES * part : LANES * part + 128] = total[:24]
-            fin_v[0, :, LANES * part + 128 : LANES * part + 256] = total[24:]
+            fin_v[0, 8:, LANES * part + 128 : LANES * part + 256] = total
+
+    def scatter_sums(stage, piece):
+        for part in range(3):
+            scatter_sum(stage, part, piece)
 
     for part in range(3):
         own = dp_v[:, pl.ds(pl.multiple_of(core * HALF + part * LANES, LANES), LANES)]
@@ -487,12 +519,9 @@
             p_v[part, mb // 2, 2 * (mb % 2) : 2 * (mb % 2) + 2] = value.astype(BF).reshape(
                 2, 4, 2, 48, 128
             )
-        scatter_start(0, part)
-
-    each_column(lambda cols: output_strips(flat_v, send_o, cols, low))
-    halo_o = halo(send_o, came_o, 2, 1)
-    for copy in halo_o:
-        copy.start()
+        scatter_start(0, part, 0)
+    for part in range(3):
+        scatter_start(0, part, 1)
 
     def d_mixed_step(n, _):
         dmix_v[n] = dot(dp_v[...], pw_v[columns_of(n), :], 1, 1).astype(BF)
@@ -530,7 +559,10 @@
             u_v[g * 4 + 2 * t + 1] = sums[1]
         return 0
 
-    lax.fori_loop(0, GROUPS, backward_step, 0)
+    lax.fori_loop(0, 4, backward_step, 0)
+    scatter_sums(0, 0)
+    lax.fori_loop(4, GROUPS, backward_step, 0)
+    scatter_sums(0, 1)
 
     small = None
     for cj in range(8):
@@ -575,56 +607,31 @@
 
     sum_start(sm_v, sm_send, sm_recv, 0, small)
 
+    def squares_place(stage):
+        return (at["x"], at["y"], at["z"] * 2 + core)[stage]
+
     def squares_copies(stage):
-        copies = []
-        if stage == 1:
-            mine = sq1_v.at[at["x"] * 4 + at["y"]]
-            for k in range(1, 16):
-                chip = dict(at)
-                chip["x"] = lax.rem(at["x"] + k // 4, 4)
-                chip["y"] = lax.rem(at["y"] + k % 4, 4)
-                copies.append(
-                    remote(mine, mine, sq_send.at[0, k - 1], sq_recv.at[0, k - 1], device(chip, core))
-                )
-        else:
-            mine = sq2_v.at[at["z"] * 2 + core]
-            for k in range(1, 8):
-                chip = dict(at)
-                chip["z"] = lax.rem(at["z"] + k // 2, 4)
-                on_core = core if k % 2 == 0 else 1 - core
-                copies.append(
-                    remote(mine, mine, sq_send.at[1, k - 1], sq_recv.at[1, k - 1], device(chip, on_core))
-                )
-        return copies
+        mine = sq_v.at[stage, squares_place(stage)]
+        return [
+            remote(mine, mine, sq_send.at[stage, i], sq_recv.at[stage, i], target)
+            for i, target in enumerate(circles[stage])
+        ]
 
     def squares_start(stage, value):
-        if stage == 1:
-            sq1_v[at["x"] * 4 + at["y"]] = value
-        else:
-            sq2_v[at["z"] * 2 + core] = value
+        sq_v[stage, squares_place(stage)] = value
         for copy in squares_copies(stage):
             copy.start()
 
     def squares_finish(stage):
         for copy in squares_copies(stage):
             copy.wait()
-        buffer, count = (sq1_v, 16) if stage == 1 else (sq2_v, 8)
-        total = buffer[0]
-        for k in range(1, count):
-            total = total + buffer[k]
+        total = sq_v[stage, 0]
+        for k in range(1, 4 if stage < 2 else 8):
+            total = total + sq_v[stage, k]
         return total
 
     def halo_d(n):
-        cols = columns_of(n)
-        rows = (slice(0, 48), slice(48, 96), slice(96, 112))
-        targets = (shifted(0, 1), shifted(1, 0), shifted(1, 1))
-        return [
-            remote(
-                send_d.at[rows[i], cols], came_d.at[rows[i], cols],
-                last_send.at[n, i], last_recv.at[n, i], targets[i],
-            )
-            for i in range(3)
-        ]
+        return halo(send_d, came_d, 3 + n, 1, columns_of(n))
 
     def store_d(n):
         cols = columns_of(n)
@@ -640,7 +647,7 @@
     def d_token_step(n, _):
         cols = columns_of(n)
         flat_v[:, cols] = c_v[:, cols].astype(F32) + dot(dqkv_v[...], w_v[cols, :], 1, 1)
-        output_strips(flat_v, send_d, cols, low)
+        output_strips(flat_v, send_d, cols)
         for copy in halo_d(n):
             copy.start()
         return 0
@@ -651,26 +658,25 @@
     store_out = pltpu.make_async_copy(oblk_v, out_h, store_sem.at[0])
     store_out.start()
 
-    for part in range(3):
-        scatter_sum(0, part)
-    lax.fori_loop(0, 2, d_token_step, 0)
+    scatter_sums(1, 0)
+    lax.fori_loop(0, 1, d_token_step, 0)
     sum_start(sm_v, sm_send, sm_recv, 1, sum_finish(sm_v, sm_send, sm_recv, 0))
-    for part in range(3):
-        scatter_sum(1, part)
-    lax.fori_loop(2, 4, d_token_step, 0)
-    sum_start(sm_v, sm_send, sm_recv, 2, sum_finish(sm_v, sm_send, sm_recv, 1))
-    for part in range(3):
-        scatter_sum(2, part)
+    scatter_sums(1, 1)
+    scatter_sums(2, 0)
+    lax.fori_loop(1, 3, d_token_step, 0)
+    scatter_sums(2, 1)
     fin_copy = remote(fin_v.at[0], fin_v.at[1], fin_sem.at[0], fin_sem.at[1], sibling)
     fin_copy.start()
     squares = fin_v[0] * fin_v[0]
     squares = squares[:8] + squares[8:16] + squares[16:]
     squares = sum(squares[:, 128 * n : 128 * n + 128] for n in range(6))
-    squares_start(1, squares)
+    squares_start(0, squares)
+    sum_start(sm_v, sm_send, sm_recv, 2, sum_finish(sm_v, sm_send, sm_recv, 1))
+    lax.fori_loop(3, 4, d_token_step, 0)
+    squares_start(1, squares_finish(0))
+    sum_start(sm_v, sm_send, sm_recv, 3, sum_finish(sm_v, sm_send, sm_recv, 2))
     lax.fori_loop(4, 6, d_token_step, 0)
-    sum_start(sm_v, sm_send, sm_recv, 3, sum_finish(sm_v, sm_send, sm_recv, 2))
-    squares = squares_finish(1)
-    squares_start(2, squares)
+    squares_start(2, squares_finish(1))
     lax.fori_loop(0, GROUPS, last_step, 0)
 
     small = sum_finish(sm_v, sm_send, sm_recv, 3)
@@ -696,12 +702,16 @@
 
 
 def hand_over(*refs):
-    sems = refs[12]
-    copies = [pltpu.make_async_copy(refs[i], refs[6 + i], sems.at[i]) for i in range(6)]
-    for copy in copies:
-        copy.start()
-    for copy in copies:
-        copy.wait()
+    source, target, held, load_sem, store_sem = refs[:6], refs[6:12], refs[12:18], refs[18], refs[19]
+    loads = [pltpu.make_async_copy(source[i], held[i], load_sem.at[i]) for i in range(6)]
+    stores = [pltpu.make_async_copy(held[i], target[i], store_sem.at[i]) for i in range(6)]
+    for load in loads:
+        load.start()
+    for load, store in zip(loads, stores):
+        load.wait()
+        store.start()
+    for store in stores:
+        store.wait()
 
 
 def on_device(tokens, qkv_weight, rel_bias, proj_weight, norm_gain, norm_shift, cotangent):
@@ -753,25 +763,22 @@
         pltpu.VMEM((3, 3, 48, 128), F32),
         pltpu.VMEM((2, 24, HALF), F32),
         pltpu.VMEM((4, 4, 40, LANES), F32),
-        pltpu.VMEM((16, 8, 128), F32),
-        pltpu.VMEM((8, 8, 128), F32),
+        pltpu.VMEM((3, 8, 8, 128), F32),
         dma((3,)),
         dma((18,)),
         dma((1,)),
-        dma((3, 3)),
-        dma((3, 3)),
+        dma((3 + GROUPS, 4)),
+        dma((3 + GROUPS, 4)),
         dma((GROUPS,)),
         dma((GROUPS,)),
         dma((WINDOWS,)),
         dma((WINDOWS,)),
-        dma((3, 3, 3)),
-        dma((3, 3, 3)),
+        dma((3, 3, 6)),
+        dma((3, 3, 6)),
         dma((4, 3)),
         dma((4, 3)),
-        dma((2, 15)),
-        dma((2, 15)),
-        dma((GROUPS, 3)),
-        dma((GROUPS, 3)),
+        dma((3, 7)),
+        dma((3, 7)),
         dma((GROUPS,)),
         dma((2,)),
     ]
@@ -800,7 +807,7 @@
         out_shape=tuple(jax.ShapeDtypeStruct(r.shape, r.dtype) for r in results),
         in_specs=[anywhere] * 6,
         out_specs=(anywhere,) * 6,
-        scratch_shapes=[dma((6,))],
+        scratch_shapes=[pltpu.VMEM(r.shape, r.dtype) for r in results] + [dma((6,)), dma((6,))],
         compiler_params=pltpu.CompilerParams(vmem_limit_bytes=60 * 2**20),
         name="hand_over",
     )(*results)

time: 131 us -> 72.4 us (0.55)
  Pallas kernels: 129 us -> 71.6 us
    pallas_call x1, Pallas kernels: 55.6 us -> 2.44 us  [on_device(): pl.pallas_call(hand_over, out_shape=tuple((jax.ShapeDtypeStruct(r.shape,...]
    pallas_call x1, Pallas kernels: 73.3 us -> 69.2 us  [on_device(): pl.pallas_call(sublayer, out_shape=(jax.ShapeDtypeStruct((16, 16, D), BF)...]
where the time goes in v3:
time: 72.4 us; the launch traced here: 72.3 us
  Pallas kernels  71.6 us (99%)
    pallas_call x1, Pallas kernels, on_device(): pl.pallas_call(sublayer, out_shape=(jax.ShapeDtypeStruct((16, 16, D), BF)...  69.2 us
    pallas_call x1, Pallas kernels, on_device(): pl.pallas_call(hand_over, out_shape=tuple((jax.ShapeDtypeStruct(r.shape,...  2.44 us

profile of v3, /device:TPU:0, one launch (start us, length us, event | category | flops | bytes accessed | tf_op | source)
XLA Modules:
  0.0 72.3 jit_solution(6057353046420415518)
XLA Ops:
  0.6 69.2 %sublayer.1 = (bf16[16,16,1536]{2,1,0:T(8,128)(2,1)}, bf16[16,16,1536]{2,1,0:T(8,128)(2,1)}, f32[12,1536]{1,0:T(8,128)}, f32[15,15,24]{2,1,0:T(8,128)}, f32[1536]{0:T(1024)}, /*index=5*/f32[1536]{0:T(1024)}) custom-call(bf16[16,16,1536]{2,1,0:T(8,128)(2,1)} %tok_h.1, bf16[1536,4608]{1,0:T(8,128)(2,1)} %wq_h.1, f32[15,15,24]{2,1,0:T(8,128)} %bitcast.2, ...), custom_call_target="tpu_custom_call" | custom-call | tf_op jit(solution)/shard_map/sublayer/pallas_call | solution.py:785
  69.8 2.4 %hand_over.1 = (bf16[16,16,1536]{2,1,0:T(8,128)(2,1)}, bf16[16,16,1536]{2,1,0:T(8,128)(2,1)}, f32[12,1536]{1,0:T(8,128)}, f32[15,15,24]{2,1,0:T(8,128)}, f32[1536]{0:T(1024)}, /*index=5*/f32[1536]{0:T(1024)}) custom-call(bf16[16,16,1536]{2,1,0:T(8,128)(2,1)} %get-tuple-element.18.refs_0_, bf16[16,16,1536]{2,1,0:T(8,128)(2,1)} %get-tuple-element.19.refs_1_, ...), custom_call_target="tpu_custom_call" | custom-call | tf_op jit(solution)/shard_map/hand_over/pallas_call | solution.py:805

commit v4 on v3

--- a/solution.py
+++ b/solution.py
@@ -194,16 +194,16 @@
 
 
 def sublayer(
-    tok_h, wq_h, rel_ref, pw_h, gain_ref, shift_ref, cot_h,
+    tok_h, wq_h, rel_h, pw_h, gain_h, shift_h, cot_h,
     out_h, dtok_h, dpw_ref, drel_ref, dgain_ref, dshift_ref,
-    tok_v, cot_v, w_v, pw_v, x_v, c_v, qkv_v, pt_v, mix_v, mixt_v, proj_v, flat_v,
+    tok_v, cot_v, w_v, pw_v, x_v, c_v, qkv_v, pt_v, mix_v, mixt_v, proj_v, flat_v, dflat_v,
     dp_v, dps_v, dmix_v, dqkv_v, oblk_v, dblk_v,
-    e_v, rel_v, gain_v, shift_v, wb_v, bt_v, mask_v, u_v, acc_v,
+    rel_ref, gain_ref, shift_ref, e_v, rel_v, gain_v, shift_v, wb_v, bt_v, mask_v, u_v, acc_v,
     send_x, came_x, send_c, came_c, send_o, came_o, send_d, came_d,
     p_v, r1a, r1c, s2a, s2b, s2c, r2a, r2b, r2c, s3a, s3b, s3c, r3, fin_v,
     sm_v, sq_v,
-    load_sem, w_sem, store_sem, halo_send, halo_recv, mix_send, mix_recv, dp_send, dp_recv,
-    rs_send, rs_recv, sm_send, sm_recv, sq_send, sq_recv, last_store, fin_sem,
+    load_sem, w_sem, store_sem, halo_send, halo_recv, mix_sem, dp_sem,
+    rs_send, rs_recv, sm_send, sm_recv, sq_send, sq_recv, fin_sem,
 ):
     lon = lax.axis_index("lon")
     lat = lax.axis_index("lat")
@@ -240,23 +240,39 @@
             device_id=target, device_id_type=MESH,
         )
 
+    def arrive(whole, send, recv):
+        group = remote(whole, whole, send, recv, sibling)
+        group.wait_send()
+        group.wait_recv()
+
     load_tok = pltpu.make_async_copy(tok_h, tok_v, load_sem.at[0])
     load_cot = pltpu.make_async_copy(cot_h, cot_v, load_sem.at[1])
     load_pw = pltpu.make_async_copy(pw_h, pw_v, load_sem.at[2])
 
     def load_w(chunk):
         cols = columns_of(chunk)
-        return pltpu.make_async_copy(wq_h.at[:, cols], w_v.at[:, cols], w_sem.at[chunk])
+        return pltpu.make_async_copy(wq_h.at[:, cols], w_v.at[:, cols], w_sem.at[lax.rem(chunk, GROUPS)])
 
     load_tok.start()
     load_cot.start()
+    loads = [
+        pltpu.make_async_copy(rel_h, rel_ref, load_sem.at[3]),
+        pltpu.make_async_copy(gain_h, gain_ref, load_sem.at[4]),
+        pltpu.make_async_copy(shift_h, shift_ref, load_sem.at[5]),
+    ]
+    for load in loads:
+        load.start()
 
     partners = [shifted(0, 1), shifted(0, -1), shifted(1, 0), shifted(-1, 0), shifted(1, -1), shifted(-1, 1)]
-    circles = [[along(axis, steps) for steps in (1, 2, 3)] for axis in "xy"]
-    circles.append(
-        [sibling] + [along("z", steps) for steps in (1, 2, 3)] + [along("z", steps, 1 - core) for steps in (1, 2, 3)]
-    )
-    partners += circles[0] + circles[1] + circles[2]
+    circles = [[], []]
+    for k in range(1, 16):
+        chip = dict(at)
+        chip["x"] = lax.rem(at["x"] + k // 4, 4)
+        chip["y"] = lax.rem(at["y"] + k % 4, 4)
+        circles[0].append(device(chip, core))
+    circles[1] += [sibling] + [along("z", steps) for steps in (1, 2, 3)]
+    circles[1] += [along("z", steps, 1 - core) for steps in (1, 2, 3)]
+    partners += circles[0] + circles[1]
     barrier = pltpu.get_barrier_semaphore()
     for partner in partners:
         pl.semaphore_signal(barrier, inc=1, device_id=partner, device_id_type=MESH)
@@ -275,7 +291,7 @@
         return [
             remote(
                 strips.at[rows, cols], came.at[rows, cols],
-                halo_send.at[which, i], halo_recv.at[which, i],
+                halo_send.at[which], halo_recv.at[which],
                 shifted(sign * STRIP_STEPS[i][0], sign * STRIP_STEPS[i][1]),
             )
             for i, rows in enumerate(STRIPS)
@@ -291,15 +307,14 @@
     load_cot.wait()
     each_column(lambda cols: input_strips(cot_v, send_c, cols, low))
     halo_c = halo(send_c, came_c, 1, -1)
-    for copy in halo_c:
-        copy.start()
-    each_column(lambda cols: own_windows(cot_v, c_v, cols, low))
 
     spot = lax.broadcasted_iota(jnp.int32, (128, LANES), 0)
     slot = lax.broadcasted_iota(jnp.int32, (128, LANES), 1)
     for cj in range(8):
         hit = ((spot >> 3) == (slot >> 4)) & ((spot & 7) - cj + 7 == (slot & 15))
         e_v[128 * cj : 128 * cj + 128, :] = jnp.where(hit, 1.0, 0.0).astype(BF)
+    for load in loads:
+        load.wait()
     rel_v[...] = jnp.zeros_like(rel_v)
     for a in range(15):
         rel_v[16 * a : 16 * a + 15, :] = rel_ref[a]
@@ -327,8 +342,9 @@
     crossing = (j_upper != i_upper) & (lat == 3)
     mask_v[...] = jnp.where(crossing, -jnp.inf, 0.0)
 
-    for copy in halo_x:
-        copy.wait()
+    arrive(came_x, halo_send.at[0], halo_recv.at[0])
+    for copy in halo_c:
+        copy.start()
     each_column(lambda cols: input_windows(tok_v, came_x, x_v, cols, low))
 
     lane_head = lax.broadcasted_iota(jnp.int32, (CELLS, LANES), 1) >> 6
@@ -337,7 +353,7 @@
     def mix_copy(g):
         rows = columns_of(g)
         return remote(
-            mixt_v.at[0, rows], mixt_v.at[1, rows], mix_send.at[g], mix_recv.at[g], sibling
+            mixt_v.at[0, rows], mixt_v.at[1, rows], mix_sem.at[0], mix_sem.at[1], sibling
         )
 
     def make_qkv(g):
@@ -349,8 +365,8 @@
             qkv_v[chunk] = value
 
     def wait_weights(g):
-        for part in range(3):
-            load_w(part * GROUPS + g).wait()
+        three = w_v.at[:, : 3 * LANES]
+        pltpu.make_async_copy(three, three, w_sem.at[g]).wait()
 
     def attend(g):
         bias = bt_v[g]
@@ -390,8 +406,8 @@
     load_pw.wait()
     lax.fori_loop(0, GROUPS, project_step, 0)
 
-    for copy in halo_c:
-        copy.wait()
+    each_column(lambda cols: own_windows(cot_v, c_v, cols, low))
+    arrive(came_c, halo_send.at[1], halo_recv.at[1])
     each_column(lambda cols: input_windows(cot_v, came_c, c_v, cols, low))
 
     acc_v[...] = jnp.zeros_like(acc_v)
@@ -404,7 +420,7 @@
 
     def dp_copy(m):
         rows = pl.ds(pl.multiple_of(m * CELLS, CELLS), CELLS)
-        return remote(dp_v.at[rows, other_half], dps_v.at[rows], dp_send.at[m], dp_recv.at[m], sibling)
+        return remote(dp_v.at[rows, other_half], dps_v.at[rows], dp_sem.at[0], dp_sem.at[1], sibling)
 
     def norm_step(m, _):
         sums = [None, None]
@@ -431,14 +447,11 @@
     lax.fori_loop(0, TOKENS // CELLS, norm_step, 0)
 
     each_column(lambda cols: output_strips(flat_v, send_o, cols))
-    halo_o = halo(send_o, came_o, 2, 1)
-    for copy in halo_o:
+    for copy in halo(send_o, came_o, 2, 1):
         copy.start()
 
-    for m in range(WINDOWS):
-        dp_copy(m).wait()
-    for g in range(GROUPS):
-        mix_copy(g).wait()
+    arrive(dps_v, dp_sem.at[0], dp_sem.at[1])
+    arrive(mixt_v.at[1], mix_sem.at[0], mix_sem.at[1])
 
     def slot_of(buffer, lead, axes, axis, index):
         if axis == "z":
@@ -458,7 +471,7 @@
         (r3.at[0], r3.at[1], r3.at[2]),
     )
 
-    pieces = (slice(0, 32), slice(32, 48))
+    pieces = (slice(0, 32), slice(32, 48), slice(0, 48))
 
     def scatter_copies(stage, part, piece):
         buffer, lead, axes = stages[stage][part]
@@ -472,8 +485,8 @@
                 remote(
                     slot_of(buffer, lead, axes, axis, index).at[whole + (rows,)],
                     arrivals[stage][part].at[(steps - 1,) + whole + (rows,)],
-                    rs_send.at[stage, part, 3 * piece + steps - 1],
-                    rs_recv.at[stage, part, 3 * piece + steps - 1],
+                    rs_send.at[stage, part, piece % 2],
+                    rs_recv.at[stage, part, piece % 2],
                     along(axis, steps),
                 )
             )
@@ -484,24 +497,27 @@
             copy.start()
 
     def scatter_sum(stage, part, piece):
-        for copy in scatter_copies(stage, part, piece):
-            copy.wait()
         buffer, lead, axes = stages[stage][part]
         axis = ORDERS[part][stage]
         rows = pieces[piece]
         whole = (slice(None),) * (len(axes) - (2 if axis == "z" else 1))
+        arrive(
+            arrivals[stage][part].at[(slice(None),) + whole + (rows,)],
+            rs_send.at[stage, part, piece % 2], rs_recv.at[stage, part, piece % 2],
+        )
         total = slot_of(buffer, lead, axes, axis, at[axis])[whole + (rows,)].astype(F32)
         for steps in range(3):
             total = total + arrivals[stage][part][(steps,) + whole + (rows,)].astype(F32)
         if stage < 2:
             target = stages[stage + 1][part][0]
             target[whole + (rows,)] = total.astype(target.dtype)
-            scatter_start(stage + 1, part, piece)
-        elif piece == 0:
+            if stage == 0:
+                scatter_start(1, part, piece)
+            elif piece == 1:
+                scatter_start(2, part, 2)
+        else:
             fin_v[0, :, LANES * part : LANES * part + 128] = total[:24]
-            fin_v[0, :8, LANES * part + 128 : LANES * part + 256] = total[24:]
-        else:
-            fin_v[0, 8:, LANES * part + 128 : LANES * part + 256] = total
+            fin_v[0, :, LANES * part + 128 : LANES * part + 256] = total[24:]
 
     def scatter_sums(stage, piece):
         for part in range(3):
@@ -523,13 +539,10 @@
     for part in range(3):
         scatter_start(0, part, 1)
 
-    def d_mixed_step(n, _):
-        dmix_v[n] = dot(dp_v[...], pw_v[columns_of(n), :], 1, 1).astype(BF)
-        return 0
-
-    lax.fori_loop(0, GROUPS, d_mixed_step, 0)
-
-    def backward_step(g, _):
+    def make_d_mixed(g):
+        dmix_v[g] = dot(dp_v[...], pw_v[columns_of(g), :], 1, 1).astype(BF)
+
+    def backward(g):
         total = None
         for w in range(WINDOWS):
             rows = slice(CELLS * w, CELLS * w + CELLS)
@@ -557,11 +570,17 @@
                 sums = [b if a is None else a + b for a, b in zip(sums, pair)]
             u_v[g * 4 + 2 * t] = sums[0]
             u_v[g * 4 + 2 * t + 1] = sums[1]
+
+    def backward_step(g, _):
+        backward(g)
+        make_d_mixed(g + 1)
         return 0
 
-    lax.fori_loop(0, 4, backward_step, 0)
+    make_d_mixed(0)
+    lax.fori_loop(0, GROUPS - 1, backward_step, 0)
+    backward(GROUPS - 1)
+
     scatter_sums(0, 0)
-    lax.fori_loop(4, GROUPS, backward_step, 0)
     scatter_sums(0, 1)
 
     small = None
@@ -580,13 +599,13 @@
     def sum_copies(buffer, send, recv, stage):
         if stage == 0:
             return [remote(
-                buffer.at[0, core], buffer.at[0, core], send.at[0, 0], recv.at[0, 0], sibling
+                buffer.at[0, core], buffer.at[0, core], send.at[0], recv.at[0], sibling
             )]
         axis = "xyz"[stage - 1]
         return [
             remote(
                 buffer.at[stage, at[axis]], buffer.at[stage, at[axis]],
-                send.at[stage, steps - 1], recv.at[stage, steps - 1], along(axis, steps),
+                send.at[stage], recv.at[stage], along(axis, steps),
             )
             for steps in (1, 2, 3)
         ]
@@ -598,8 +617,7 @@
             copy.start()
 
     def sum_finish(buffer, send, recv, stage):
-        for copy in sum_copies(buffer, send, recv, stage):
-            copy.wait()
+        arrive(buffer.at[stage, slice(0, 1 if stage == 0 else 3)], send.at[stage], recv.at[stage])
         total = buffer[stage, 0] + buffer[stage, 1]
         if stage > 0:
             total = total + buffer[stage, 2] + buffer[stage, 3]
@@ -608,13 +626,13 @@
     sum_start(sm_v, sm_send, sm_recv, 0, small)
 
     def squares_place(stage):
-        return (at["x"], at["y"], at["z"] * 2 + core)[stage]
+        return (at["x"] * 4 + at["y"], at["z"] * 2 + core)[stage]
 
     def squares_copies(stage):
         mine = sq_v.at[stage, squares_place(stage)]
         return [
-            remote(mine, mine, sq_send.at[stage, i], sq_recv.at[stage, i], target)
-            for i, target in enumerate(circles[stage])
+            remote(mine, mine, sq_send.at[stage], sq_recv.at[stage], target)
+            for target in circles[stage]
         ]
 
     def squares_start(stage, value):
@@ -623,10 +641,10 @@
             copy.start()
 
     def squares_finish(stage):
-        for copy in squares_copies(stage):
-            copy.wait()
+        count = (16, 8)[stage]
+        arrive(sq_v.at[stage, slice(0, count - 1)], sq_send.at[stage], sq_recv.at[stage])
         total = sq_v[stage, 0]
-        for k in range(1, 4 if stage < 2 else 8):
+        for k in range(1, count):
             total = total + sq_v[stage, k]
         return total
 
@@ -635,36 +653,28 @@
 
     def store_d(n):
         cols = columns_of(n)
-        return pltpu.make_async_copy(dblk_v.at[:, :, cols], dtok_h.at[:, :, cols], last_store.at[n])
+        return pltpu.make_async_copy(dblk_v.at[:, :, cols], dtok_h.at[:, :, cols], store_sem.at[1])
 
     def last_step(n, _):
-        for copy in halo_d(n):
-            copy.wait()
-        output_block(flat_v, came_d, dblk_v, columns_of(n), low)
+        arrive(came_d.at[:, columns_of(n)], halo_send.at[3 + n], halo_recv.at[3 + n])
+        output_block(dflat_v, came_d, dblk_v, columns_of(n), low)
         store_d(n).start()
         return 0
 
     def d_token_step(n, _):
         cols = columns_of(n)
-        flat_v[:, cols] = c_v[:, cols].astype(F32) + dot(dqkv_v[...], w_v[cols, :], 1, 1)
-        output_strips(flat_v, send_d, cols)
+        dflat_v[:, cols] = c_v[:, cols].astype(F32) + dot(dqkv_v[...], w_v[cols, :], 1, 1)
+        output_strips(dflat_v, send_d, cols)
         for copy in halo_d(n):
             copy.start()
         return 0
 
-    for copy in halo_o:
-        copy.wait()
-    each_column(lambda cols: output_block(flat_v, came_o, oblk_v, cols, low))
-    store_out = pltpu.make_async_copy(oblk_v, out_h, store_sem.at[0])
-    store_out.start()
-
+    lax.fori_loop(0, 1, d_token_step, 0)
     scatter_sums(1, 0)
-    lax.fori_loop(0, 1, d_token_step, 0)
+    scatter_sums(1, 1)
     sum_start(sm_v, sm_send, sm_recv, 1, sum_finish(sm_v, sm_send, sm_recv, 0))
-    scatter_sums(1, 1)
-    scatter_sums(2, 0)
-    lax.fori_loop(1, 3, d_token_step, 0)
-    scatter_sums(2, 1)
+    lax.fori_loop(1, 4, d_token_step, 0)
+    scatter_sums(2, 2)
     fin_copy = remote(fin_v.at[0], fin_v.at[1], fin_sem.at[0], fin_sem.at[1], sibling)
     fin_copy.start()
     squares = fin_v[0] * fin_v[0]
@@ -672,15 +682,17 @@
     squares = sum(squares[:, 128 * n : 128 * n + 128] for n in range(6))
     squares_start(0, squares)
     sum_start(sm_v, sm_send, sm_recv, 2, sum_finish(sm_v, sm_send, sm_recv, 1))
-    lax.fori_loop(3, 4, d_token_step, 0)
+    lax.fori_loop(4, 6, d_token_step, 0)
     squares_start(1, squares_finish(0))
     sum_start(sm_v, sm_send, sm_recv, 3, sum_finish(sm_v, sm_send, sm_recv, 2))
-    lax.fori_loop(4, 6, d_token_step, 0)
-    squares_start(2, squares_finish(1))
+    arrive(came_o, halo_send.at[2], halo_recv.at[2])
+    each_column(lambda cols: output_block(flat_v, came_o, oblk_v, cols, low))
+    store_out = pltpu.make_async_copy(oblk_v, out_h, store_sem.at[0])
+    store_out.start()
     lax.fori_loop(0, GROUPS, last_step, 0)
 
     small = sum_finish(sm_v, sm_send, sm_recv, 3)
-    squares = squares_finish(2)
+    squares = squares_finish(1)
     total = jnp.sum(squares, axis=(0, 1), keepdims=True)
     total = total + jnp.sum(small * small, axis=(0, 1), keepdims=True)
     factor = jnp.minimum(1.0, jnp.sqrt(PARAMS / (total + clip_epsilon)))
@@ -697,8 +709,7 @@
     dpw_ref[:, :HALF] = jnp.where(core == 0, own, other)
     dpw_ref[:, HALF:] = jnp.where(core == 0, other, own)
     store_out.wait()
-    for n in range(GROUPS):
-        store_d(n).wait()
+    pltpu.make_async_copy(dblk_v, dtok_h, store_sem.at[1]).wait()
 
 
 def hand_over(*refs):
@@ -732,12 +743,16 @@
         pltpu.VMEM((2, D, TOKENS), BF),
         pltpu.VMEM((TOKENS, D), F32),
         pltpu.VMEM((TOKENS, D), F32),
+        pltpu.VMEM((TOKENS, D), F32),
         pltpu.VMEM((TOKENS, D), BF),
         pltpu.VMEM((TOKENS, HALF), BF),
         pltpu.VMEM((GROUPS, TOKENS, LANES), BF),
         pltpu.VMEM((TOKENS, 3 * D), BF),
         pltpu.VMEM((16, 16, D), BF),
         pltpu.VMEM((16, 16, D), BF),
+        pltpu.VMEM((15, 15, HEADS), F32),
+        pltpu.VMEM((D,), F32),
+        pltpu.VMEM((D,), F32),
         pltpu.VMEM((1024, LANES), BF),
         pltpu.VMEM((LANES, HEADS), F32),
         pltpu.VMEM((1, D), F32),
@@ -763,23 +778,20 @@
         pltpu.VMEM((3, 3, 48, 128), F32),
         pltpu.VMEM((2, 24, HALF), F32),
         pltpu.VMEM((4, 4, 40, LANES), F32),
-        pltpu.VMEM((3, 8, 8, 128), F32),
-        dma((3,)),
-        dma((18,)),
-        dma((1,)),
-        dma((3 + GROUPS, 4)),
-        dma((3 + GROUPS, 4)),
+        pltpu.VMEM((2, 16, 8, 128), F32),
+        dma((6,)),
         dma((GROUPS,)),
-        dma((GROUPS,)),
-        dma((WINDOWS,)),
-        dma((WINDOWS,)),
-        dma((3, 3, 6)),
-        dma((3, 3, 6)),
-        dma((4, 3)),
-        dma((4, 3)),
-        dma((3, 7)),
-        dma((3, 7)),
-        dma((GROUPS,)),
+        dma((2,)),
+        dma((3 + GROUPS,)),
+        dma((3 + GROUPS,)),
+        dma((2,)),
+        dma((2,)),
+        dma((3, 3, 2)),
+        dma((3, 3, 2)),
+        dma((4,)),
+        dma((4,)),
+        dma((2,)),
+        dma((2,)),
         dma((2,)),
     ]
     results = pl.pallas_call(
@@ -792,7 +804,7 @@
             jax.ShapeDtypeStruct((D,), F32),
             jax.ShapeDtypeStruct((D,), F32),
         ),
-        in_specs=[anywhere, anywhere, vmem, anywhere, vmem, vmem, anywhere],
+        in_specs=[anywhere] * 7,
         out_specs=(anywhere, anywhere, vmem, vmem, vmem, vmem),
         scratch_shapes=scratch,
         compiler_params=pltpu.CompilerParams(

time: 72.4 us -> 66.7 us (0.921)
  Pallas kernels: 71.6 us -> 65.9 us
    pallas_call x1, Pallas kernels: 69.2 us -> 63.5 us  [on_device(): pl.pallas_call(sublayer, out_shape=(jax.ShapeDtypeStruct((16, 16, D), BF)...]
where the time goes in v4:
time: 66.7 us; the launch traced here: 66.6 us
  Pallas kernels  65.9 us (99%)
    pallas_call x1, Pallas kernels, on_device(): pl.pallas_call(sublayer, out_shape=(jax.ShapeDtypeStruct((16, 16, D), BF)...  63.5 us
    pallas_call x1, Pallas kernels, on_device(): pl.pallas_call(hand_over, out_shape=tuple((jax.ShapeDtypeStruct(r.shape,...  2.44 us

profile of v4, /device:TPU:0, one launch (start us, length us, event | category | flops | bytes accessed | tf_op | source)
XLA Modules:
  0.0 66.6 jit_solution(1735292694506659105)
XLA Ops:
  0.6 63.5 %sublayer.1 = (bf16[16,16,1536]{2,1,0:T(8,128)(2,1)}, bf16[16,16,1536]{2,1,0:T(8,128)(2,1)}, f32[12,1536]{1,0:T(8,128)}, f32[15,15,24]{2,1,0:T(8,128)}, f32[1536]{0:T(1024)}, /*index=5*/f32[1536]{0:T(1024)}) custom-call(bf16[16,16,1536]{2,1,0:T(8,128)(2,1)} %tok_h.1, bf16[1536,4608]{1,0:T(8,128)(2,1)} %wq_h.1, f32[15,15,24]{2,1,0:T(8,128)} %bitcast.2, ...), custom_call_target="tpu_custom_call" | custom-call | tf_op jit(solution)/shard_map/sublayer/pallas_call | solution.py:797
  64.1 2.4 %hand_over.1 = (bf16[16,16,1536]{2,1,0:T(8,128)(2,1)}, bf16[16,16,1536]{2,1,0:T(8,128)(2,1)}, f32[12,1536]{1,0:T(8,128)}, f32[15,15,24]{2,1,0:T(8,128)}, f32[1536]{0:T(1024)}, /*index=5*/f32[1536]{0:T(1024)}) custom-call(bf16[16,16,1536]{2,1,0:T(8,128)(2,1)} %get-tuple-element.18.refs_0_, bf16[16,16,1536]{2,1,0:T(8,128)(2,1)} %get-tuple-element.19.refs_1_, ...), custom_call_target="tpu_custom_call" | custom-call | tf_op jit(solution)/shard_map/hand_over/pallas_call | solution.py:817

commit v5 on v4

--- a/solution.py
+++ b/solution.py
@@ -249,9 +249,9 @@
     load_cot = pltpu.make_async_copy(cot_h, cot_v, load_sem.at[1])
     load_pw = pltpu.make_async_copy(pw_h, pw_v, load_sem.at[2])
 
-    def load_w(chunk):
-        cols = columns_of(chunk)
-        return pltpu.make_async_copy(wq_h.at[:, cols], w_v.at[:, cols], w_sem.at[lax.rem(chunk, GROUPS)])
+    def load_w(g, part):
+        source = wq_h.at[:, columns_of(part * GROUPS + g)]
+        return pltpu.make_async_copy(source, w_v.at[:, columns_of(3 * g + part)], w_sem.at[g])
 
     load_tok.start()
     load_cot.start()
@@ -279,7 +279,7 @@
 
     for g in range(GROUPS):
         for part in range(3):
-            load_w(part * GROUPS + g).start()
+            load_w(g, part).start()
     load_pw.start()
 
     low = low_rows(LANES)
@@ -357,12 +357,12 @@
         )
 
     def make_qkv(g):
+        whole = dot(x_v[...], w_v[:, columns_of(g, HALF)], 1, 0).astype(BF)
         for part in range(3):
-            chunk = part * GROUPS + g
-            value = dot(x_v[...], w_v[:, columns_of(chunk)], 1, 0).astype(BF)
+            value = whole[:, LANES * part : LANES * part + LANES]
             if part == 0:
                 value = value * jnp.asarray(0.125, BF)
-            qkv_v[chunk] = value
+            qkv_v[part * GROUPS + g] = value
 
     def wait_weights(g):
         three = w_v.at[:, : 3 * LANES]
@@ -399,12 +399,12 @@
     mix_copy(GROUPS - 1).start()
 
     def project_step(n, _):
-        cols = columns_of(n)
+        cols = columns_of(n, HALF)
         proj_v[:, cols] = dot(mix_v[...], pw_v[:, cols], 1, 0)
         return 0
 
     load_pw.wait()
-    lax.fori_loop(0, GROUPS, project_step, 0)
+    lax.fori_loop(0, 2, project_step, 0)
 
     each_column(lambda cols: own_windows(cot_v, c_v, cols, low))
     arrive(came_c, halo_send.at[1], halo_recv.at[1])
@@ -471,57 +471,46 @@
         (r3.at[0], r3.at[1], r3.at[2]),
     )
 
-    pieces = (slice(0, 32), slice(32, 48), slice(0, 48))
-
-    def scatter_copies(stage, part, piece):
+    def scatter_copies(stage, part):
         buffer, lead, axes = stages[stage][part]
         axis = ORDERS[part][stage]
-        rows = pieces[piece]
-        whole = (slice(None),) * (len(axes) - (2 if axis == "z" else 1))
         copies = []
         for steps in (1, 2, 3):
             index = lax.rem(at[axis] + steps, 4)
             copies.append(
                 remote(
-                    slot_of(buffer, lead, axes, axis, index).at[whole + (rows,)],
-                    arrivals[stage][part].at[(steps - 1,) + whole + (rows,)],
-                    rs_send.at[stage, part, piece % 2],
-                    rs_recv.at[stage, part, piece % 2],
+                    slot_of(buffer, lead, axes, axis, index),
+                    arrivals[stage][part].at[steps - 1],
+                    rs_send.at[stage, part],
+                    rs_recv.at[stage, part],
                     along(axis, steps),
                 )
             )
         return copies
 
-    def scatter_start(stage, part, piece):
-        for copy in scatter_copies(stage, part, piece):
+    def scatter_start(stage, part):
+        for copy in scatter_copies(stage, part):
             copy.start()
 
-    def scatter_sum(stage, part, piece):
+    def scatter_sum(stage, part):
         buffer, lead, axes = stages[stage][part]
         axis = ORDERS[part][stage]
-        rows = pieces[piece]
-        whole = (slice(None),) * (len(axes) - (2 if axis == "z" else 1))
-        arrive(
-            arrivals[stage][part].at[(slice(None),) + whole + (rows,)],
-            rs_send.at[stage, part, piece % 2], rs_recv.at[stage, part, piece % 2],
-        )
-        total = slot_of(buffer, lead, axes, axis, at[axis])[whole + (rows,)].astype(F32)
+        came = arrivals[stage][part]
+        arrive(came, rs_send.at[stage, part], rs_recv.at[stage, part])
+        total = slot_of(buffer, lead, axes, axis, at[axis])[...].astype(F32)
         for steps in range(3):
-            total = total + arrivals[stage][part][(steps,) + whole + (rows,)].astype(F32)
+            total = total + came[steps].astype(F32)
         if stage < 2:
             target = stages[stage + 1][part][0]
-            target[whole + (rows,)] = total.astype(target.dtype)
-            if stage == 0:
-                scatter_start(1, part, piece)
-            elif piece == 1:
-                scatter_start(2, part, 2)
+            target[...] = total.astype(target.dtype)
+            scatter_start(stage + 1, part)
         else:
             fin_v[0, :, LANES * part : LANES * part + 128] = total[:24]
             fin_v[0, :, LANES * part + 128 : LANES * part + 256] = total[24:]
 
-    def scatter_sums(stage, piece):
+    def scatter_sums(stage):
         for part in range(3):
-            scatter_sum(stage, part, piece)
+            scatter_sum(stage, part)
 
     for part in range(3):
         own = dp_v[:, pl.ds(pl.multiple_of(core * HALF + part * LANES, LANES), LANES)]
@@ -535,9 +524,7 @@
             p_v[part, mb // 2, 2 * (mb % 2) : 2 * (mb % 2) + 2] = value.astype(BF).reshape(
                 2, 4, 2, 48, 128
             )
-        scatter_start(0, part, 0)
-    for part in range(3):
-        scatter_start(0, part, 1)
+        scatter_start(0, part)
 
     def make_d_mixed(g):
         dmix_v[g] = dot(dp_v[...], pw_v[columns_of(g), :], 1, 1).astype(BF)
@@ -557,7 +544,7 @@
             dk = dot(low_scores, block_diagonal(q, lane_head), 1, 0)
             dv = dot(shares.astype(BF), d_out, 1, 0)
             for part, value in enumerate((dq, dk, dv)):
-                dqkv_v[rows, columns_of(part * GROUPS + g)] = value.astype(BF)
+                dqkv_v[rows, columns_of(3 * g + part)] = value.astype(BF)
         for t in range(2):
             sums = [None, None]
             for rj in range(8):
@@ -579,9 +566,6 @@
     make_d_mixed(0)
     lax.fori_loop(0, GROUPS - 1, backward_step, 0)
     backward(GROUPS - 1)
-
-    scatter_sums(0, 0)
-    scatter_sums(0, 1)
 
     small = None
     for cj in range(8):
@@ -649,32 +633,32 @@
         return total
 
     def halo_d(n):
-        return halo(send_d, came_d, 3 + n, 1, columns_of(n))
+        return halo(send_d, came_d, 3 + n, 1, columns_of(n, 512))
 
     def store_d(n):
-        cols = columns_of(n)
+        cols = columns_of(n, 512)
         return pltpu.make_async_copy(dblk_v.at[:, :, cols], dtok_h.at[:, :, cols], store_sem.at[1])
 
     def last_step(n, _):
-        arrive(came_d.at[:, columns_of(n)], halo_send.at[3 + n], halo_recv.at[3 + n])
-        output_block(dflat_v, came_d, dblk_v, columns_of(n), low)
+        arrive(came_d.at[:, columns_of(n, 512)], halo_send.at[3 + n], halo_recv.at[3 + n])
+        output_block(dflat_v, came_d, dblk_v, columns_of(n, 512), low_rows(512))
         store_d(n).start()
         return 0
 
     def d_token_step(n, _):
-        cols = columns_of(n)
+        cols = columns_of(n, 512)
         dflat_v[:, cols] = c_v[:, cols].astype(F32) + dot(dqkv_v[...], w_v[cols, :], 1, 1)
         output_strips(dflat_v, send_d, cols)
         for copy in halo_d(n):
             copy.start()
         return 0
 
+    scatter_sums(0)
     lax.fori_loop(0, 1, d_token_step, 0)
-    scatter_sums(1, 0)
-    scatter_sums(1, 1)
+    scatter_sums(1)
     sum_start(sm_v, sm_send, sm_recv, 1, sum_finish(sm_v, sm_send, sm_recv, 0))
-    lax.fori_loop(1, 4, d_token_step, 0)
-    scatter_sums(2, 2)
+    lax.fori_loop(1, 3, d_token_step, 0)
+    scatter_sums(2)
     fin_copy = remote(fin_v.at[0], fin_v.at[1], fin_sem.at[0], fin_sem.at[1], sibling)
     fin_copy.start()
     squares = fin_v[0] * fin_v[0]
@@ -682,32 +666,32 @@
     squares = sum(squares[:, 128 * n : 128 * n + 128] for n in range(6))
     squares_start(0, squares)
     sum_start(sm_v, sm_send, sm_recv, 2, sum_finish(sm_v, sm_send, sm_recv, 1))
-    lax.fori_loop(4, 6, d_token_step, 0)
-    squares_start(1, squares_finish(0))
-    sum_start(sm_v, sm_send, sm_recv, 3, sum_finish(sm_v, sm_send, sm_recv, 2))
     arrive(came_o, halo_send.at[2], halo_recv.at[2])
     each_column(lambda cols: output_block(flat_v, came_o, oblk_v, cols, low))
     store_out = pltpu.make_async_copy(oblk_v, out_h, store_sem.at[0])
     store_out.start()
-    lax.fori_loop(0, GROUPS, last_step, 0)
+    squares_start(1, squares_finish(0))
+    sum_start(sm_v, sm_send, sm_recv, 3, sum_finish(sm_v, sm_send, sm_recv, 2))
+    lax.fori_loop(0, 3, last_step, 0)
 
     small = sum_finish(sm_v, sm_send, sm_recv, 3)
+    small_total = jnp.sum(small * small, axis=(0, 1), keepdims=True)
+    drel = small[:24].T
+    fin_copy.wait()
+    own = jnp.where(core == 0, fin_v[0, :12], fin_v[0, 12:])
+    other = jnp.where(core == 0, fin_v[1, :12], fin_v[1, 12:])
+    first, second = jnp.where(core == 0, own, other), jnp.where(core == 0, other, own)
     squares = squares_finish(1)
-    total = jnp.sum(squares, axis=(0, 1), keepdims=True)
-    total = total + jnp.sum(small * small, axis=(0, 1), keepdims=True)
+    total = jnp.sum(squares, axis=(0, 1), keepdims=True) + small_total
     factor = jnp.minimum(1.0, jnp.sqrt(PARAMS / (total + clip_epsilon)))
-    drel = (small[:24] * factor).T
+    dpw_ref[:, :HALF] = first * factor
+    dpw_ref[:, HALF:] = second * factor
+    drel = drel * factor
     for a in range(15):
         drel_ref[a] = drel[16 * a : 16 * a + 15]
     for n in range(GROUPS):
         dgain_ref[LANES * n : LANES * n + LANES] = (small[24 + n : 25 + n] * factor).reshape(LANES)
         dshift_ref[LANES * n : LANES * n + LANES] = (small[32 + n : 33 + n] * factor).reshape(LANES)
-    fin_copy.wait()
-    own, other = fin_v[0] * factor, fin_v[1] * factor
-    own = jnp.where(core == 0, own[:12], own[12:])
-    other = jnp.where(core == 0, other[:12], other[12:])
-    dpw_ref[:, :HALF] = jnp.where(core == 0, own, other)
-    dpw_ref[:, HALF:] = jnp.where(core == 0, other, own)
     store_out.wait()
     pltpu.make_async_copy(dblk_v, dtok_h, store_sem.at[1]).wait()
 
@@ -772,22 +756,22 @@
         pltpu.VMEM((3, 2, 2, 48, 128), BF),
         pltpu.VMEM((3, 4, 48, 128), BF),
         pltpu.VMEM((3, 4, 48, 128), BF),
-        pltpu.VMEM((2, 2, 48, 128), F32),
-        pltpu.VMEM((4, 48, 128), F32),
-        pltpu.VMEM((4, 48, 128), F32),
-        pltpu.VMEM((3, 3, 48, 128), F32),
+        pltpu.VMEM((2, 2, 48, 128), BF),
+        pltpu.VMEM((4, 48, 128), BF),
+        pltpu.VMEM((4, 48, 128), BF),
+        pltpu.VMEM((3, 3, 48, 128), BF),
         pltpu.VMEM((2, 24, HALF), F32),
         pltpu.VMEM((4, 4, 40, LANES), F32),
         pltpu.VMEM((2, 16, 8, 128), F32),
         dma((6,)),
         dma((GROUPS,)),
         dma((2,)),
-        dma((3 + GROUPS,)),
-        dma((3 + GROUPS,)),
+        dma((6,)),
+        dma((6,)),
         dma((2,)),
         dma((2,)),
-        dma((3, 3, 2)),
-        dma((3, 3, 2)),
+        dma((3, 3)),
+        dma((3, 3)),
         dma((4,)),
         dma((4,)),
         dma((2,)),

time: 66.7 us -> 65.6 us (0.984)
  Pallas kernels: 65.9 us -> 64.8 us
    pallas_call x1, Pallas kernels: 63.5 us -> 62.4 us  [on_device(): pl.pallas_call(sublayer, out_shape=(jax.ShapeDtypeStruct((16, 16, D), BF)...]
where the time goes in v5:
time: 65.6 us; the launch traced here: 65.4 us
  Pallas kernels  64.8 us (99%)
    pallas_call x1, Pallas kernels, on_device(): pl.pallas_call(sublayer, out_shape=(jax.ShapeDtypeStruct((16, 16, D), BF)...  62.4 us
    pallas_call x1, Pallas kernels, on_device(): pl.pallas_call(hand_over, out_shape=tuple((jax.ShapeDtypeStruct(r.shape,...  2.44 us

profile of v5, /device:TPU:0, one launch (start us, length us, event | category | flops | bytes accessed | tf_op | source)
XLA Modules:
  0.0 65.4 jit_solution(7548042173838911987)
XLA Ops:
  0.6 62.4 %sublayer.1 = (bf16[16,16,1536]{2,1,0:T(8,128)(2,1)}, bf16[16,16,1536]{2,1,0:T(8,128)(2,1)}, f32[12,1536]{1,0:T(8,128)}, f32[15,15,24]{2,1,0:T(8,128)}, f32[1536]{0:T(1024)}, /*index=5*/f32[1536]{0:T(1024)}) custom-call(bf16[16,16,1536]{2,1,0:T(8,128)(2,1)} %tok_h.1, bf16[1536,4608]{1,0:T(8,128)(2,1)} %wq_h.1, f32[15,15,24]{2,1,0:T(8,128)} %bitcast.2, ...), custom_call_target="tpu_custom_call" | custom-call | tf_op jit(solution)/shard_map/sublayer/pallas_call | solution.py:781
  63.0 2.4 %hand_over.1 = (bf16[16,16,1536]{2,1,0:T(8,128)(2,1)}, bf16[16,16,1536]{2,1,0:T(8,128)(2,1)}, f32[12,1536]{1,0:T(8,128)}, f32[15,15,24]{2,1,0:T(8,128)}, f32[1536]{0:T(1024)}, /*index=5*/f32[1536]{0:T(1024)}) custom-call(bf16[16,16,1536]{2,1,0:T(8,128)(2,1)} %get-tuple-element.18.refs_0_, bf16[16,16,1536]{2,1,0:T(8,128)(2,1)} %get-tuple-element.19.refs_1_, ...), custom_call_target="tpu_custom_call" | custom-call | tf_op jit(solution)/shard_map/hand_over/pallas_call | solution.py:801

commit v6 on v5

--- a/solution.py
+++ b/solution.py
@@ -585,7 +585,7 @@
             return [remote(
                 buffer.at[0, core], buffer.at[0, core], send.at[0], recv.at[0], sibling
             )]
-        axis = "xyz"[stage - 1]
+        axis = "zxy"[stage - 1]
         return [
             remote(
                 buffer.at[stage, at[axis]], buffer.at[stage, at[axis]],
@@ -595,7 +595,7 @@
         ]
 
     def sum_start(buffer, send, recv, stage, value):
-        place = core if stage == 0 else at["xyz"[stage - 1]]
+        place = core if stage == 0 else at["zxy"[stage - 1]]
         buffer[stage, place] = value
         for copy in sum_copies(buffer, send, recv, stage):
             copy.start()
@@ -664,6 +664,7 @@
     squares = fin_v[0] * fin_v[0]
     squares = squares[:8] + squares[8:16] + squares[16:]
     squares = sum(squares[:, 128 * n : 128 * n + 128] for n in range(6))
+    squares = jnp.sum(squares, axis=0, keepdims=True)
     squares_start(0, squares)
     sum_start(sm_v, sm_send, sm_recv, 2, sum_finish(sm_v, sm_send, sm_recv, 1))
     arrive(came_o, halo_send.at[2], halo_recv.at[2])
@@ -762,7 +763,7 @@
         pltpu.VMEM((3, 3, 48, 128), BF),
         pltpu.VMEM((2, 24, HALF), F32),
         pltpu.VMEM((4, 4, 40, LANES), F32),
-        pltpu.VMEM((2, 16, 8, 128), F32),
+        pltpu.VMEM((2, 16, 1, 128), F32),
         dma((6,)),
         dma((GROUPS,)),
         dma((2,)),

time: 65.6 us -> 65.8 us (level)
  no operation moved by 1% of the time
where the time goes in v6:
time: 65.8 us; the launch traced here: 65.6 us
  Pallas kernels  65 us (99%)
    pallas_call x1, Pallas kernels, on_device(): pl.pallas_call(sublayer, out_shape=(jax.ShapeDtypeStruct((16, 16, D), BF)...  62.6 us
    pallas_call x1, Pallas kernels, on_device(): pl.pallas_call(hand_over, out_shape=tuple((jax.ShapeDtypeStruct(r.shape,...  2.44 us

profile of v6, /device:TPU:0, one launch (start us, length us, event | category | flops | bytes accessed | tf_op | source)
XLA Modules:
  0.0 65.6 jit_solution(13675383211076997280)
XLA Ops:
  0.6 62.6 %sublayer.1 = (bf16[16,16,1536]{2,1,0:T(8,128)(2,1)}, bf16[16,16,1536]{2,1,0:T(8,128)(2,1)}, f32[12,1536]{1,0:T(8,128)}, f32[15,15,24]{2,1,0:T(8,128)}, f32[1536]{0:T(1024)}, /*index=5*/f32[1536]{0:T(1024)}) custom-call(bf16[16,16,1536]{2,1,0:T(8,128)(2,1)} %tok_h.1, bf16[1536,4608]{1,0:T(8,128)(2,1)} %wq_h.1, f32[15,15,24]{2,1,0:T(8,128)} %bitcast.2, ...), custom_call_target="tpu_custom_call" | custom-call | tf_op jit(solution)/shard_map/sublayer/pallas_call | solution.py:782
  63.2 2.4 %hand_over.1 = (bf16[16,16,1536]{2,1,0:T(8,128)(2,1)}, bf16[16,16,1536]{2,1,0:T(8,128)(2,1)}, f32[12,1536]{1,0:T(8,128)}, f32[15,15,24]{2,1,0:T(8,128)}, f32[1536]{0:T(1024)}, /*index=5*/f32[1536]{0:T(1024)}) custom-call(bf16[16,16,1536]{2,1,0:T(8,128)(2,1)} %get-tuple-element.18.refs_0_, bf16[16,16,1536]{2,1,0:T(8,128)(2,1)} %get-tuple-element.19.refs_1_, ...), custom_call_target="tpu_custom_call" | custom-call | tf_op jit(solution)/shard_map/hand_over/pallas_call | solution.py:802
